TPU v7x, 256 devices: a whole 4x4x8 slice. The times are simulated.
256 devices in a mesh: ctx: 64 (over z_hi, y, x), tp: 4 (over z_lo, core).
Axes of the slice: x: 4, y: 4, z: 8 (z_hi: 4, z_lo: 2; z = z_hi * 2 + z_lo), core: 2. Of those that a mesh axis runs over, the one named last changes fastest.
Arguments:
- q_dec: bfloat16 [2, 512, 5120], P(None, 'ctx', 'tp')
- k_dec: bfloat16 [2, 512, 5120], P(None, 'ctx', 'tp'), may hold values from -8 to 8
- v_dec: bfloat16 [2, 512, 5120], P(None, 'ctx', 'tp')
- ctx_k: bfloat16 [2, 16384, 5120], P(None, 'ctx', 'tp')
- ctx_v: bfloat16 [2, 16384, 5120], P(None, 'ctx', 'tp')
- lengths: int32 [2], replicated, may hold values from 4096 to 16384, as said below
- gain: float32 [5120], P('tp'), may hold values from 0.5 to 1.5
Outputs:
- attn_out: bfloat16 [2, 512, 5120], P(None, 'ctx', 'tp')
Inputs may be any that keep to these rules, and one draw needn't show every extreme that they name: `lengths`: context positions at or past a sequence's length are unused; in every draw some sequence uses all 16384 positions.
All inputs are finite; a program needn't handle non-finite values.
Results may differ from a plain program's by a relative error of at most 0.011.
Values may be sent and summed in bfloat16 or wider, within the bound.
A program may use at most 64 MiB of HBM per device.

v0:
```python
import jax
import jax.numpy as jnp
from jax import lax
from jax.sharding import PartitionSpec as P

DH = 128


def per_device(q_dec, k_dec, v_dec, ctx_k, ctx_v, lengths, gain):
    seq_count, block_rows, feature_width = q_dec.shape
    head_count = feature_width // DH
    cache_rows = ctx_k.shape[1]
    my_rank = lax.axis_index("ctx")
    queries = lax.all_gather(q_dec, "ctx", axis=1, tiled=True)
    total_rows = queries.shape[1]
    local_rows = jnp.arange(cache_rows, dtype=jnp.int32)
    cache_k, cache_v = (ctx_k, ctx_v)
    positions = my_rank * cache_rows + local_rows
    key_block = min(128, cache_rows)
    scaling = DH ** (-0.5)
    numer_list, total_list, peak_list = ([], [], [])
    for sequence in range(seq_count):
        query_rows = queries[sequence].reshape(total_rows, head_count, DH)
        own_keys = k_dec[sequence].reshape(block_rows, head_count, DH)
        own_values = v_dec[sequence].reshape(block_rows, head_count, DH)
        scores = (
            jnp.einsum("qhd,khd->hqk", query_rows, own_keys, preferred_element_type=jnp.float32)
            * scaling
        )
        row_peak = jnp.max(scores, axis=2)
        weights = jnp.exp(scores - row_peak[..., None])
        row_total = jnp.sum(weights, axis=2)
        numerator = jnp.einsum(
            "hqk,khd->hqd",
            weights.astype(jnp.bfloat16),
            own_values,
            preferred_element_type=jnp.float32,
        )
        running = (row_peak, row_total, numerator)
        length_now = lengths[sequence]
        for block in range(cache_rows // key_block):
            lower = block * key_block
            block_keys = cache_k[sequence, lower : lower + key_block].reshape(
                key_block, head_count, DH
            )
            block_values = cache_v[sequence, lower : lower + key_block].reshape(
                key_block, head_count, DH
            )
            is_valid = positions[lower : lower + key_block] < length_now

            def absorb(
                carried, block_keys=block_keys, block_values=block_values, is_valid=is_valid
            ):
                old_peak, old_total, old_numer = carried
                block_scores = (
                    jnp.einsum(
                        "qhd,khd->hqk", query_rows, block_keys, preferred_element_type=jnp.float32
                    )
                    * scaling
                )
                block_scores = jnp.where(is_valid[None, None, :], block_scores, -jnp.inf)
                new_peak = jnp.maximum(old_peak, jnp.max(block_scores, axis=2))
                correction = jnp.exp(old_peak - new_peak)
                block_weights = jnp.exp(block_scores - new_peak[..., None])
                new_total = old_total * correction + jnp.sum(block_weights, axis=2)
                new_numer = old_numer * correction[..., None] + jnp.einsum(
                    "hqk,khd->hqd",
                    block_weights.astype(jnp.bfloat16),
                    block_values,
                    preferred_element_type=jnp.float32,
                )
                return (new_peak, new_total, new_numer)

            def unchanged(carried):
                return carried

            running = lax.cond(positions[lower] < length_now, absorb, unchanged, running)
        row_peak, row_total, numerator = running
        numer_list.append(numerator.transpose(1, 0, 2).reshape(total_rows, feature_width))
        total_list.append(row_total.T)
        peak_list.append(row_peak.T)
    numer_all = jnp.stack(numer_list)
    total_all = jnp.stack(total_list)
    peak_all = jnp.stack(peak_list)
    global_peak = lax.pmax(peak_all.astype(jnp.bfloat16), "ctx").astype(peak_all.dtype)
    factor = jnp.exp(peak_all - global_peak)
    scaled = (numer_all.reshape(seq_count, total_rows, head_count, DH) * factor[..., None]).reshape(
        seq_count, total_rows, feature_width
    )
    summed_flat, norm_sum = (
        lax.psum_scatter(scaled, "ctx", scatter_dimension=1, tiled=True),
        lax.psum_scatter(total_all * factor, "ctx", scatter_dimension=1, tiled=True),
    )
    summed = summed_flat.reshape(seq_count, block_rows, head_count, DH)
    attended = (summed / norm_sum[..., None]).reshape(seq_count, block_rows, feature_width)
    squares = jnp.sum(attended * attended, axis=-1)
    total_sq = lax.psum(squares, "tp")
    mean_sq = total_sq / (feature_width * lax.axis_size("tp"))
    return (attended * lax.rsqrt(mean_sq + 1e-06)[..., None] * gain).astype(jnp.bfloat16)


def solution(mesh):
    return jax.shard_map(
        per_device,
        mesh=mesh,
        in_specs=(
            P(None, "ctx", "tp"),
            P(None, "ctx", "tp"),
            P(None, "ctx", "tp"),
            P(None, "ctx", "tp"),
            P(None, "ctx", "tp"),
            P(),
            P("tp"),
        ),
        out_specs=P(None, "ctx", "tp"),
        check_vma=False,
    )
```

profile of v0, /device:TPU:1, one launch (start us, length us, event | category | flops | bytes accessed | tf_op | source)
XLA Modules:
  0.0 1308.7 jit_solution(6899099868548547236)
XLA Ops:
  6.5 1.5 copy.169
  8.2 1.3 fusion.63
  19.4 75.1 %all-gather.2.cloned.1.call-done = bf16[2,512,1280]{2,0,1:T(2,128)(2,1)} async-done(((bf16[2,8,1280]{2,0,1:T(2,128)(2,1)}), bf16[2,512,1280]{2,0,1:T(2,128)(2,1)}) %all-gather.2.cloned.1.call-update) | async-done | bytes 2621456 | tf_op jit(solution)/shard_map/all_gather | solution.py:14
  94.5 8.2 fusion.59
  102.7 4.9 copy.215
  107.7 5.3 copy.218
  113.9 2.1 fusion.44
  116.6 6.7 conditional.6
  116.6 2.0 fusion.20
  119.4 4.0 multiply_add_fusion.4
  123.9 14.3 %conditional.7 = ((f32[10,512]{1,0:T(8,128)S(1)}, f32[10,512]{1,0:T(8,128)S(1)}, f32[10,512,128]{2,1,0:T(8,128)})) conditional(s32[]{:T(128)} %convert_element_type.42, (f32[10,512]{1,0:T(8,128)S(1)}, f32[10,512]{1,0:T(8,128)S(1)}, f32[10,512,128]{2,1,0:T(8,128)}) %get-tuple-element.363, (s32[128]{0:T(128)S(1)}, s32[128]{0:T(128)S(1)}, ...), branch_computations={%region_16.17_spmd, %region_17.20_spmd} | conditional | flops 344074368 | bytes 23266876 | solution.py:77
  124.0 2.4 copy.190
  126.4 1.7 slice.87
  128.1 2.4 copy.188
  131.6 2.0 fusion.30
  134.2 4.0 multiply_add_fusion.6
  138.2 3.2 copy.191
  141.5 4.6 conditional.4
  141.7 2.0 fusion
  144.3 1.8 multiply_add_fusion
  146.7 11.3 conditional.5
  146.7 2.4 copy.179
  150.1 2.4 copy.177
  153.6 2.0 fusion.10
  156.2 1.8 multiply_add_fusion.2
  158.0 2.2 copy.180
  160.2 316.5 %pmax.7 = bf16[2,512,10]{1,0,2:T(2,128)(2,1)S(1)} all-reduce(bf16[2,512,10]{1,0,2:T(2,128)(2,1)S(1)} %fusion.58), channel_id=1, replica_groups=mesh['ctx'=64,'tp'=4] {'ctx'}, use_global_device_ids=true, to_apply=%region_20.21 | all-reduce | flops 10240 | bytes 40960 | tf_op jit(solution)/shard_map/pmax | solution.py:85
  476.8 5.5 maximum_multiply_fusion
  482.4 9.0 copy.193
  493.5 328.7 %all-reduce.1 = f32[2,512,10]{2,0,1:T(2,128)S(1)} all-reduce(f32[2,512,10]{2,0,1:T(2,128)S(1)} %copy.194), channel_id=3, replica_groups=mesh['ctx'=64,'tp'=4] {'ctx'}, use_global_device_ids=true, to_apply=%region_22.23.clone | all-reduce | flops 10240 | bytes 81920
  822.3 430.6 %all-reduce.4.cloned.1.call-done = f32[2,512,1280]{2,0,1:T(2,128)} async-done(((f32[2,512,1280]{2,0,1:T(2,128)}), f32[2,512,1280]{2,0,1:T(2,128)}) %all-reduce.4.cloned.1.call-update) | async-done | bytes 5242896
  1254.0 47.2 %psum.7 = f32[2,8]{1,0:T(2,128)S(1)} all-reduce(f32[2,8]{1,0:T(2,128)S(1)} %multiply_reduce_fusion), channel_id=1, replica_groups=mesh['ctx'=64,'tp'=4] {'tp'}, use_global_device_ids=true, to_apply=%region_24.25 | all-reduce | flops 16 | bytes 128 | tf_op jit(solution)/shard_map/psum | solution.py:97
  (75 shorter events, 17.0 us)
Async XLA Ops:
  6.5 10.6 copy-start.2
  6.5 88.0 %all-gather.2.cloned.1.call-start = ((), (), s32[]{:S(2)}) async-start(), calls=%async_computation | async-start | bytes 2662400 | tf_op jit(solution)/shard_map/all_gather | solution.py:14
  8.1 1244.8 %all-reduce.4.cloned.1.call-start = ((), (), s32[]{:S(2)}) async-start(), calls=%async_computation.1 | async-start | bytes 10485760
  107.7 5.7 copy-start
  107.7 5.4 copy-start.6
  113.0 2.9 copy-start.1
  113.0 0.8 copy-start.5
  116.6 2.7 copy-start.3
  131.5 2.7 copy-start.4
  491.3 0.7 copy-start.8
  491.3 809.8 %copy-start.7 = (f32[1280]{0:T(1024)S(1)}, f32[1280]{0:T(1024)}, u32[]{:S(2)}) copy-start(f32[1280]{0:T(1024)} %param.21) | copy-start | bytes 15364
Sparse Core Ops, SparseCore 0:
  10.7 83.8 all-gather.1
  491.5 761.3 all-reduce.3
where the time goes:
time: 1310 us
  blocking collectives  692 us (53%)
  waiting for transfers between devices  506 us (39%)
  local copies, waits for them, and re-layouts  57.9 us (4%)
  matrix products  22.7 us (2%)
  between operations  19.1 us (1%)
    unnamed x3, waiting for transfers between devices  431 us
    unnamed x1, blocking collectives  329 us
    pmax x1, blocking collectives, per_device(): lax.pmax(peak_all.astype(jnp.bfloat16), 'ctx').astype(peak_all.dtype)  316 us
    all_gather x1, waiting for transfers between devices, per_device(): queries = lax.all_gather(q_dec, 'ctx', axis=1, tiled=True)  75.1 us
    psum x1, blocking collectives, per_device(): total_sq = lax.psum(squares, 'tp')  47.2 us
  transfers between devices with their start and end apart: 2, of which 2 were waited for; matrix products, arithmetic and copies ran while one was open for 1% of the time, Pallas kernels for 0%

commit v1 on v0

v1 whole, which is shorter than its diff:
```python
import functools
import math

import jax
import jax.numpy as jnp
from jax import lax
from jax.experimental import pallas as pl
from jax.experimental.pallas import tpu as pltpu
from jax.sharding import PartitionSpec as P

MESH = pl.DeviceIdType.MESH
DH = 128
HEADS = 10
CHUNKS = ((0, 4), (4, 4), (8, 2))
ORDER = (("z", "y", "x"), ("z", "x", "y"), ("x", "y", "z"))
STRIDE = {"z": 16, "y": 4, "x": 1}
F32 = jnp.float32
BF16 = jnp.bfloat16
NT = (((1,), (1,)), ((), ()))


def kernel(
    q_ref, kd_ref, vd_ref, ck_ref, cv_ref, len_ref, gain_ref, out_ref,
    qbuf, sbuf, r1, s2, r2, s3, r3, st1, rs1, st2, rs2, st3, rs3, fbuf, ftbuf, nsend, nrecv,
    kbuf, vbuf, vt, kdp, vdt, bias,
    a1s, a1r, a2s, a2r, a3s, a3r, r1s, r1r, t1s, t1r, r2s, r2r, t2s, t2r, r3s, r3r, t3s, t3r, ns, nr, kvsem,
):
    ctx = lax.axis_index("ctx")
    tp = lax.axis_index("tp")
    pos = {name: (ctx // STRIDE[name]) % 4 for name in "zyx"}

    def peer(name, off):
        return (ctx + ((pos[name] + off) % 4 - pos[name]) * STRIDE[name], tp)

    kv_copies = []
    for s in range(2):
        kv_copies.append(pltpu.make_async_copy(ck_ref.at[s], kbuf.at[s], kvsem.at[0, s]))
        kv_copies.append(pltpu.make_async_copy(cv_ref.at[s], vbuf.at[s], kvsem.at[1, s]))
    for copy in kv_copies:
        copy.start()

    barrier = pltpu.get_barrier_semaphore()
    for off in (1, 2, 3):
        for name in "zyx":
            pl.semaphore_signal(barrier, inc=1, device_id=peer(name, off), device_id_type=MESH)
        pl.semaphore_signal(barrier, inc=1, device_id=(ctx, (tp + off) % 4), device_id_type=MESH)

    own = q_ref[...].astype(F32).reshape(16, HEADS * DH).astype(BF16)
    place = []
    for k, (first, count) in enumerate(CHUNKS):
        a, b, c = (pos[name] for name in ORDER[k])
        place.append((a, b, c))
        for h in range(first, first + count):
            qbuf[h, c, b, a] = own[:, h * DH : (h + 1) * DH]

    pl.semaphore_wait(barrier, 12)

    def remote(src, dst, send, recv, target):
        return pltpu.make_async_remote_copy(
            src_ref=src, dst_ref=dst, send_sem=send, recv_sem=recv, device_id=target, device_id_type=MESH
        )

    sent = []

    def a1(k, off):
        first, count = CHUNKS[k]
        a, b, c = place[k]
        block = qbuf.at[pl.ds(first, count), c, b, a]
        return remote(block, block, a1s.at[k, off - 1], a1r.at[k, off - 1], peer(ORDER[k][0], off))

    def a2(k, off):
        first, count = CHUNKS[k]
        a, b, c = place[k]
        block = qbuf.at[pl.ds(first, count), c, b]
        return remote(block, block, a2s.at[k, off - 1], a2r.at[k, off - 1], peer(ORDER[k][1], off))

    for k in range(3):
        for off in (1, 3, 2):
            copy = a1(k, off)
            copy.start()
            sent.append(copy)

    row = lax.broadcasted_iota(jnp.int32, (256, DH), 0)
    dec_row = lax.broadcasted_iota(jnp.int32, (16, DH), 0)
    for s in range(2):
        limit = len_ref[s] - ctx * 256
        bias[s, 0:256] = jnp.where(row < limit, 0.0, -jnp.inf).astype(F32)
        bias[s, 256:272] = jnp.where(dec_row < 8, 0.0, -jnp.inf).astype(F32)
        pad = jnp.zeros((8, HEADS * DH), F32)
        kdp[s] = jnp.concatenate([kd_ref[s].astype(F32), pad], axis=0).astype(BF16)
        vpad = jnp.concatenate([vd_ref[s].astype(F32), jnp.zeros((DH - 8, HEADS * DH), F32)], axis=0)
        for h in range(HEADS):
            vdt[h, s] = vpad[:, h * DH : (h + 1) * DH].T.astype(BF16)
    for k in range(3):
        for off in range(4):
            st1[k, off] = jnp.zeros((8, DH), F32)

    for copy in kv_copies:
        copy.wait()

    def wait_a1(k):
        for off in (1, 3, 2):
            a1(k, off).wait_recv()
        for off in (1, 3, 2):
            copy = a2(k, off)
            copy.start()
            sent.append(copy)

    for k in range(3):
        wait_a1(k)

    @pl.loop(0, HEADS)
    def _(h):
        lanes = pl.ds(pl.multiple_of(h * DH, DH), DH)
        for s in range(2):
            vt[h, s] = vbuf[s, :, lanes].astype(F32).T.astype(BF16)

    def a3(h, off, stride, here):
        block = qbuf.at[h, here]
        target = (ctx + ((here + off) % 4 - here) * stride, tp)
        return remote(block, block, a3s.at[h, off - 1], a3r.at[h, off - 1], target)

    for k in range(3):
        first, count = CHUNKS[k]
        for off in (1, 3, 2):
            a2(k, off).wait_recv()
        for h in range(first, first + count):
            for off in (1, 3, 2):
                a3(h, off, STRIDE[ORDER[k][2]], place[k][2]).start()

    scale = math.log2(math.e) / math.sqrt(DH)

    def attend(k, h, j, off, here):
        lanes = pl.ds(pl.multiple_of(h * DH, DH), DH)
        quarter = (here + 4 - off) % 4
        rows = qbuf[h, quarter].reshape(16, 16, DH).astype(F32)
        for s in range(2):
            q = rows[:, 8 * s : 8 * s + 8, :].reshape(DH, DH).astype(BF16)
            x0 = lax.dot_general(kbuf[s, :, lanes], q, NT, preferred_element_type=F32) * scale + bias[s, 0:256]
            x1 = lax.dot_general(kdp[s, :, lanes], q, NT, preferred_element_type=F32) * scale + bias[s, 256:272]
            peak = jnp.maximum(jnp.max(x0, axis=0, keepdims=True), jnp.max(x1, axis=0, keepdims=True))
            w0 = jnp.exp2(x0 - peak)
            w1 = jnp.exp2(x1 - peak)
            total = jnp.sum(w0, axis=0, keepdims=True) + jnp.sum(w1, axis=0, keepdims=True)
            numer = jnp.dot(vt[h, s], w0.astype(BF16), preferred_element_type=F32)
            numer += jnp.dot(vdt[h, s, :, 0:16], w1.astype(BF16), preferred_element_type=F32)
            sbuf[h, off, s] = (numer * (1.0 / total)).astype(BF16)
            st1[k, off, pl.ds(2 * j + s, 1)] = peak + jnp.log2(total)

    def r1c(h, off, stride, here):
        target = (ctx + ((here + 4 - off) % 4 - here) * stride, tp)
        return remote(sbuf.at[h, off], r1.at[h, off - 1], r1s.at[h, off - 1], r1r.at[h, off - 1], target)

    @pl.loop(0, HEADS)
    def _(t):
        k = (t % 5) % 3
        j = (t // 5) * (2 - k // 2) + (t % 5) // 3
        h = 4 * k + j
        stride = 1 + 3 * k + 9 * (k * (k - 1) // 2)
        here = (ctx // stride) % 4
        for off in (0, 1, 3, 2):
            if off:
                a3(h, off, stride, here).wait_recv()
            attend(k, h, j, off, here)
            if off:
                r1c(h, off, stride, here).start()

    def stat1(k, off):
        return remote(st1.at[k, off], rs1.at[k, off - 1], t1s.at[k, off - 1], t1r.at[k, off - 1], peer(ORDER[k][2], 4 - off))

    for k in range(3):
        for off in (1, 3, 2):
            copy = stat1(k, off)
            copy.start()
            sent.append(copy)

    def merge(parts):
        peak = functools.reduce(jnp.maximum, parts)
        weights = [jnp.exp2(part - peak) for part in parts]
        total = functools.reduce(jnp.add, weights)
        inverse = 1.0 / total
        return [w * inverse for w in weights], peak + jnp.log2(total)

    def second(k, off):
        first, count = CHUNKS[k]
        name = ORDER[k][1]
        there = (pos[name] + off) % 4
        return (
            remote(
                s2.at[there, pl.ds(first, count)], r2.at[off - 1, pl.ds(first, count)],
                r2s.at[k, off - 1], r2r.at[k, off - 1], peer(name, off),
            ),
            remote(st2.at[k], rs2.at[k, off - 1], t2s.at[k, off - 1], t2r.at[k, off - 1], peer(name, off)),
        )

    for k, (first, count) in enumerate(CHUNKS):
        for off in (1, 3, 2):
            stat1(k, off).wait_recv()
        factors, log_total = merge([st1[k, 0]] + [rs1[k, off - 1] for off in (1, 2, 3)])
        st2[k] = log_total
        for i in range(4):
            fbuf[k, i] = factors[i]

        @pl.loop(0, count)
        def _(j, k=k, first=first):
            h = first + j
            stride, here = STRIDE[ORDER[k][2]], place[k][2]
            for off in (1, 3, 2):
                r1c(h, off, stride, here).wait_recv()
            for s in range(2):
                at = pl.ds(2 * j + s, 1)
                acc = sbuf[h, 0, s].astype(F32) * fbuf[k, 0, at]
                for off in (1, 2, 3):
                    acc += r1[h, off - 1, s].astype(F32) * fbuf[k, off, at]
                rows = acc.T.astype(BF16)
                for i in range(4):
                    s2[i, h, s] = rows[32 * i : 32 * i + 32]

        for off in (1, 3, 2):
            for copy in second(k, off):
                copy.start()
                sent.append(copy)

    def third(k, off):
        first, count = CHUNKS[k]
        name = ORDER[k][0]
        there = (pos[name] + off) % 4
        return (
            remote(
                s3.at[there, pl.ds(first, count)], r3.at[off - 1, pl.ds(first, count)],
                r3s.at[k, off - 1], r3r.at[k, off - 1], peer(name, off),
            ),
            remote(st3.at[k], rs3.at[k, off - 1], t3s.at[k, off - 1], t3r.at[k, off - 1], peer(name, off)),
        )

    blank = jnp.zeros((DH - 32, DH), F32)
    for k, (first, count) in enumerate(CHUNKS):
        a, b, c = place[k]
        for off in (1, 3, 2):
            for copy in second(k, off):
                copy.wait_recv()
        factors, log_total = merge([st2[k]] + [rs2[k, off - 1] for off in (1, 2, 3)])
        st3[k] = log_total
        ftbuf[k] = jnp.concatenate(factors + [blank], axis=0).T
        fr = ftbuf[k, pl.ds(pl.multiple_of(b * 32, 32), 32)]
        for j in range(count):
            h = first + j
            merged = []
            for s in range(2):
                col = 2 * j + s
                acc = s2[b, h, s].astype(F32) * fr[:, col : col + 1]
                for off in (1, 2, 3):
                    acc += r2[off - 1, h, s].astype(F32) * fr[:, 8 * off + col : 8 * off + col + 1]
                merged.append(acc)
            for i in range(4):
                s3[i, h] = jnp.concatenate([m[8 * i : 8 * i + 8] for m in merged], axis=0).astype(BF16)
        for off in (1, 3, 2):
            for copy in third(k, off):
                copy.start()
                sent.append(copy)

    attended = []
    for k, (first, count) in enumerate(CHUNKS):
        a, b, c = place[k]
        for off in (1, 3, 2):
            for copy in third(k, off):
                copy.wait_recv()
        factors, _ = merge([st3[k]] + [rs3[k, off - 1] for off in (1, 2, 3)])
        ftbuf[3 + k] = jnp.concatenate(factors + [blank], axis=0).T
        fr = ftbuf[3 + k, pl.ds(pl.multiple_of(b * 32 + a * 8, 8), 8)]
        for j in range(count):
            h = first + j

            def column(i, j=j, fr=fr):
                return jnp.concatenate([fr[:, i * 8 + 2 * j + s : i * 8 + 2 * j + s + 1] for s in range(2)], axis=0)

            acc = s3[a, h].astype(F32) * column(0)
            for off in (1, 2, 3):
                acc += r3[off - 1, h].astype(F32) * column(off)
            attended.append(acc)

    squares = functools.reduce(jnp.add, [x * x for x in attended])
    nsend[...] = squares

    def norm(off):
        return remote(nsend, nrecv.at[off - 1], ns.at[off - 1], nr.at[off - 1], (ctx, (tp + off) % 4))

    for off in (1, 2, 3):
        copy = norm(off)
        copy.start()
        sent.append(copy)
    for off in (1, 2, 3):
        norm(off).wait_recv()
    squares = squares + nrecv[0] + nrecv[1] + nrecv[2]
    mean = jnp.sum(squares, axis=1, keepdims=True) * (1.0 / (4 * HEADS * DH))
    inverse = lax.rsqrt(mean + 1e-06)
    for h in range(HEADS):
        y = attended[h] * inverse * gain_ref[:, h * DH : (h + 1) * DH]
        for s in range(2):
            out_ref[s, :, h * DH : (h + 1) * DH] = y[8 * s : 8 * s + 8].astype(BF16)

    for copy in sent:
        copy.wait_send()
    for k, (first, count) in enumerate(CHUNKS):
        for h in range(first, first + count):
            for off in (1, 3, 2):
                a3(h, off, STRIDE[ORDER[k][2]], place[k][2]).wait_send()
                r1c(h, off, STRIDE[ORDER[k][2]], place[k][2]).wait_send()


def per_device(q_dec, k_dec, v_dec, ctx_k, ctx_v, lengths, gain):
    dma = pltpu.SemaphoreType.DMA
    vmem = pl.BlockSpec(memory_space=pltpu.VMEM)
    hbm = pl.BlockSpec(memory_space=pl.ANY)
    scratch = [
        pltpu.VMEM((HEADS, 4, 4, 4, 16, DH), BF16),
        pltpu.VMEM((HEADS, 4, 2, DH, DH), BF16),
        pltpu.VMEM((HEADS, 3, 2, DH, DH), BF16),
        pltpu.VMEM((4, HEADS, 2, 32, DH), BF16),
        pltpu.VMEM((3, HEADS, 2, 32, DH), BF16),
        pltpu.VMEM((4, HEADS, 16, DH), BF16),
        pltpu.VMEM((3, HEADS, 16, DH), BF16),
        pltpu.VMEM((3, 4, 8, DH), F32),
        pltpu.VMEM((3, 3, 8, DH), F32),
        pltpu.VMEM((3, 8, DH), F32),
        pltpu.VMEM((3, 3, 8, DH), F32),
        pltpu.VMEM((3, 8, DH), F32),
        pltpu.VMEM((3, 3, 8, DH), F32),
        pltpu.VMEM((3, 4, 8, DH), F32),
        pltpu.VMEM((6, DH, DH), F32),
        pltpu.VMEM((16, DH), F32),
        pltpu.VMEM((3, 16, DH), F32),
        pltpu.VMEM((2, 256, HEADS * DH), BF16),
        pltpu.VMEM((2, 256, HEADS * DH), BF16),
        pltpu.VMEM((HEADS, 2, DH, 256), BF16),
        pltpu.VMEM((2, 16, HEADS * DH), BF16),
        pltpu.VMEM((HEADS, 2, DH, DH), BF16),
        pltpu.VMEM((2, 272, DH), F32),
        dma((3, 3)), dma((3, 3)), dma((3, 3)), dma((3, 3)),
        dma((HEADS, 3)), dma((HEADS, 3)), dma((HEADS, 3)), dma((HEADS, 3)),
        dma((3, 3)), dma((3, 3)), dma((3, 3)), dma((3, 3)), dma((3, 3)), dma((3, 3)),
        dma((3, 3)), dma((3, 3)), dma((3, 3)), dma((3, 3)),
        dma((3,)), dma((3,)),
        dma((2, 2)),
    ]
    return pl.pallas_call(
        kernel,
        out_shape=jax.ShapeDtypeStruct(q_dec.shape, BF16),
        in_specs=[vmem, vmem, vmem, hbm, hbm, pl.BlockSpec(memory_space=pltpu.SMEM), vmem],
        out_specs=vmem,
        scratch_shapes=scratch,
        compiler_params=pltpu.CompilerParams(
            collective_id=0, has_side_effects=True, vmem_limit_bytes=48 << 20
        ),
        cost_estimate=pl.CostEstimate(flops=1_400_000_000, bytes_accessed=8_000_000, transcendentals=2_700_000),
        name="block_attention",
    )(q_dec, k_dec, v_dec, ctx_k, ctx_v, lengths, gain.reshape(1, -1))


def solution(mesh):
    return jax.shard_map(
        per_device,
        mesh=mesh,
        in_specs=(
            P(None, "ctx", "tp"),
            P(None, "ctx", "tp"),
            P(None, "ctx", "tp"),
            P(None, "ctx", "tp"),
            P(None, "ctx", "tp"),
            P(),
            P("tp"),
        ),
        out_specs=P(None, "ctx", "tp"),
        check_vma=False,
    )
```

time: 1310 us -> 80.4 us (0.06)
  blocking collectives: 692 us -> 0 us
  waiting for transfers between devices: 506 us -> 0 us
  Pallas kernels: 0 us -> 73.1 us
  local copies, waits for them, and re-layouts: 57.9 us -> 6.94 us
  matrix products: 22.7 us -> 0 us
  between operations: 19.1 us -> 0.02 us
    unnamed x3 -> x0, waiting for transfers between devices: 431 us -> none
    unnamed x1 -> x0, blocking collectives: 329 us -> none
    pmax x1 -> x0, blocking collectives: 316 us -> none  [per_device(): lax.pmax(peak_all.astype(jnp.bfloat16), 'ctx').astype(peak_all.dtype)]
    all_gather x1 -> x0, waiting for transfers between devices: 75.1 us -> none  [per_device(): queries = lax.all_gather(q_dec, 'ctx', axis=1, tiled=True)]
    pallas_call x0 -> x1, Pallas kernels: none -> 73.1 us  [per_device(): pl.pallas_call(kernel, out_shape=jax.ShapeDtypeStruct(q_dec.shape, BF16),...]
    psum x1 -> x0, blocking collectives: 47.2 us -> none  [per_device(): total_sq = lax.psum(squares, 'tp')]
    dot_general x12 -> x0, matrix products: 22.7 us -> none  [the longest x4 11.4 us: absorb(): jnp.einsum('hqk,khd->hqd', block_weights.astype(jnp.bfloat16), block_valu...]
    slice x10 -> x0, local copies, waits for them, and re-layouts: 15.9 us -> none  [the longest x1 8.21 us: per_device(): query_rows = queries[sequence].reshape(total_rows, head_count, DH)]
  transfers between devices with their start and end apart: 2 -> 0, of which waited for: 2 -> 0; matrix products, arithmetic and copies ran while one was open for 1% -> 0% of each run, Pallas kernels for 0% -> 0%
where the time goes in v1:
time: 80.4 us; the launch traced here: 80 us
  Pallas kernels  73.1 us (91%)
  local copies, waits for them, and re-layouts  6.94 us (9%)
    pallas_call x1, Pallas kernels, per_device(): pl.pallas_call(kernel, out_shape=jax.ShapeDtypeStruct(q_dec.shape, BF16),...  73.1 us
    unnamed x13, local copies, waits for them, and re-layouts  6.24 us

profile of v1, /device:TPU:1, one launch (start us, length us, event | category | flops | bytes accessed | tf_op | source)
XLA Modules:
  0.0 80.0 jit_solution(401898446506357743)
XLA Ops:
  0.0 0.7 reshape.3.gain_ref
  0.7 0.0 copy-start
  0.7 1.3 %copy-done = bf16[2,256,1280]{2,1,0:T(8,128)(2,1)S(1)} copy-done((bf16[2,256,1280]{2,1,0:T(8,128)(2,1)S(1)}, bf16[2,256,1280]{2,1,0:T(8,128)(2,1)}, u32[]{:S(2)}) %copy-start) | copy-done | bytes 1310744
  2.0 0.0 copy-start.1
  2.0 1.3 %copy-done.1 = bf16[2,256,1280]{2,1,0:T(8,128)(2,1)S(1)} copy-done((bf16[2,256,1280]{2,1,0:T(8,128)(2,1)S(1)}, bf16[2,256,1280]{2,1,0:T(8,128)(2,1)}, u32[]{:S(2)}) %copy-start.1) | copy-done | bytes 1310744
  3.3 0.0 copy-start.2
  3.3 0.8 copy-done.2
  4.1 0.0 copy-start.3
  4.1 0.8 copy-done.3
  4.9 0.0 copy-start.4
  4.9 0.8 copy-done.4
  5.7 0.0 copy-start.5
  5.7 0.7 copy-done.5
  6.3 73.1 %block_attention.1 = bf16[2,8,1280]{2,1,0:T(8,128)(2,1)S(1)} custom-call(bf16[2,8,1280]{2,1,0:T(8,128)(2,1)S(1)} %copy-done.2, bf16[2,8,1280]{2,1,0:T(8,128)(2,1)S(1)} %copy-done.3, bf16[2,8,1280]{2,1,0:T(8,128)(2,1)S(1)} %copy-done.4, bf16[2,256,1280]{2,1,0:T(8,128)(2,1)S(1)} %copy-done, bf16[2,256,1280]{2,1,0:T(8,128)(2,1)S(1)} %copy-done.1, ...), custom_call_target="tpu_custom_call" | custom-call | flops 1400000000 | bytes 8000000 | tf_op jit(solution)/shard_map/block_attention/pallas_call | solution.py:346
  79.4 0.6 copy.9
Async XLA Ops:
  0.7 1.3 %copy-start = (bf16[2,256,1280]{2,1,0:T(8,128)(2,1)S(1)}, bf16[2,256,1280]{2,1,0:T(8,128)(2,1)}, u32[]{:S(2)}) copy-start(bf16[2,256,1280]{2,1,0:T(8,128)(2,1)} %ck_ref.1) | copy-start | bytes 3932164
  2.0 1.3 %copy-start.1 = (bf16[2,256,1280]{2,1,0:T(8,128)(2,1)S(1)}, bf16[2,256,1280]{2,1,0:T(8,128)(2,1)}, u32[]{:S(2)}) copy-start(bf16[2,256,1280]{2,1,0:T(8,128)(2,1)} %cv_ref.1) | copy-start | bytes 3932164
  3.3 0.8 copy-start.2
  4.1 0.8 copy-start.3
  4.9 0.8 copy-start.4
  5.7 0.7 copy-start.5

commit v2 on v0

v2 whole, which is shorter than its diff:
```python
import functools
import math

import jax
import jax.numpy as jnp
from jax import lax
from jax.experimental import pallas as pl
from jax.experimental.pallas import tpu as pltpu
from jax.sharding import PartitionSpec as P

MESH = pl.DeviceIdType.MESH
DH = 128
HEADS = 10
CHUNKS = ((0, 4), (4, 4), (8, 2))
ORDER = (("z", "y", "x"), ("z", "x", "y"), ("x", "y", "z"))
STRIDE = {"z": 16, "y": 4, "x": 1}
F32 = jnp.float32
BF16 = jnp.bfloat16
NT = (((1,), (1,)), ((), ()))
OFFS = (1, 3, 2)
LAG1, LAG2, LAG3 = 2, 4, 6


def kernel(
    q_hbm, kd_hbm, vd_hbm, ck_hbm, cv_hbm, len_hbm, gain_hbm, out_ref,
    q_ref, kd_ref, vd_ref, kbuf, vbuf, len_ref, gain_ref,
    qbuf, s1, r1, s2, r2, s3, r3, factor, attended, nsend, nrecv, vt, kdp, vdt, bias,
    insem, a1s, a1r, a2s, a2r, a3s, a3r, r1s, r1r, r2s, r2r, r3s, r3r, ns, nr,
):
    ctx = lax.axis_index("ctx")
    tp = lax.axis_index("tp")
    pos = {name: (ctx // STRIDE[name]) % 4 for name in "zyx"}

    loads = [
        pltpu.make_async_copy(src, dst, insem.at[i])
        for i, (src, dst) in enumerate((
            (q_hbm, q_ref), (kd_hbm, kd_ref), (vd_hbm, vd_ref), (ck_hbm, kbuf), (cv_hbm, vbuf), (len_hbm, len_ref), (gain_hbm, gain_ref),
        ))
    ]
    for load in loads:
        load.start()

    def along(stride, off):
        here = (ctx // stride) % 4
        return (ctx + ((here + off) % 4 - here) * stride, tp)

    barrier = pltpu.get_barrier_semaphore()
    for off in (1, 2, 3):
        for name in "zyx":
            pl.semaphore_signal(barrier, inc=1, device_id=along(STRIDE[name], off), device_id_type=MESH)
        pl.semaphore_signal(barrier, inc=1, device_id=(ctx, (tp + off) % 4), device_id_type=MESH)

    loads[0].wait()
    own = q_ref[...].astype(F32).reshape(16, HEADS * DH).astype(BF16)
    place = []
    for k, (first, count) in enumerate(CHUNKS):
        a, b, c = (pos[name] for name in ORDER[k])
        place.append((a, b, c))
        for h in range(first, first + count):
            qbuf[h, c, b, a] = own[:, h * DH : (h + 1) * DH]

    pl.semaphore_wait(barrier, 12)

    def remote(src, dst, send, recv, target):
        return pltpu.make_async_remote_copy(
            src_ref=src, dst_ref=dst, send_sem=send, recv_sem=recv, device_id=target, device_id_type=MESH
        )

    def a1(k, off):
        first, count = CHUNKS[k]
        a, b, c = place[k]
        block = qbuf.at[pl.ds(first, count), c, b, a]
        return remote(block, block, a1s.at[k, off - 1], a1r.at[k, off - 1], along(STRIDE[ORDER[k][0]], off))

    def a2(k, off):
        first, count = CHUNKS[k]
        a, b, c = place[k]
        block = qbuf.at[pl.ds(first, count), c, b]
        return remote(block, block, a2s.at[k, off - 1], a2r.at[k, off - 1], along(STRIDE[ORDER[k][1]], off))

    for k in (2, 0, 1):
        for off in OFFS:
            a1(k, off).start()

    for load in loads[1:]:
        load.wait()
    row = lax.broadcasted_iota(jnp.int32, (256, DH), 0)
    dec_row = lax.broadcasted_iota(jnp.int32, (16, DH), 0)
    for s in range(2):
        limit = len_ref[s] - ctx * 256
        bias[s, 0:256] = jnp.where(row < limit, 0.0, -jnp.inf).astype(F32)
        bias[s, 256:272] = jnp.where(dec_row < 8, 0.0, -jnp.inf).astype(F32)
        pad = jnp.zeros((8, HEADS * DH), F32)
        kdp[s] = jnp.concatenate([kd_ref[s].astype(F32), pad], axis=0).astype(BF16)
        vpad = jnp.concatenate([vd_ref[s].astype(F32), jnp.zeros((DH - 8, HEADS * DH), F32)], axis=0)
        for h in range(HEADS):
            vdt[h, s] = vpad[:, h * DH : (h + 1) * DH].T.astype(BF16)

    for k in (2, 0, 1):
        for off in OFFS:
            a1(k, off).wait_recv()
        for off in OFFS:
            a2(k, off).start()

    @pl.loop(0, HEADS)
    def _(h):
        lanes = pl.ds(pl.multiple_of(h * DH, DH), DH)
        for s in range(2):
            vt[h, s] = vbuf[s, :, lanes].astype(F32).T.astype(BF16)

    def head_of(t):
        k = (t % 5) % 3
        return 4 * k + (t // 5) * (2 - k // 2) + (t % 5) // 3, k

    def stride_a(k):
        return 16 - 15 * (k * (k - 1) // 2)

    def stride_b(k):
        return 4 - 3 * (k * (2 - k))

    def stride_c(k):
        return 1 + 3 * k + 9 * (k * (k - 1) // 2)

    def a3(h, k, off):
        block = qbuf.at[h, (ctx // stride_c(k)) % 4]
        return remote(block, block, a3s.at[h, off - 1], a3r.at[h, off - 1], along(stride_c(k), off))

    def first_back(h, k, off):
        return remote(s1.at[h, off], r1.at[h, off - 1], r1s.at[h, off - 1], r1r.at[h, off - 1], along(stride_c(k), 4 - off))

    def second_back(h, k, off):
        there = ((ctx // stride_b(k)) % 4 + off) % 4
        return remote(s2.at[h, there], r2.at[h, off - 1], r2s.at[h, off - 1], r2r.at[h, off - 1], along(stride_b(k), off))

    def third_back(h, k, off):
        there = ((ctx // stride_a(k)) % 4 + off) % 4
        return remote(s3.at[h, there], r3.at[h, off - 1], r3s.at[h, off - 1], r3r.at[h, off - 1], along(stride_a(k), off))

    for k in (2, 0, 1):
        first, count = CHUNKS[k]
        for off in OFFS:
            a2(k, off).wait_recv()
        for h in range(first, first + count):
            for off in OFFS:
                a3(h, k, off).start()

    scale = math.log2(math.e) / math.sqrt(DH)

    def split(lse):
        high = lse.astype(BF16).astype(F32)
        middle = (lse - high).astype(BF16).astype(F32)
        low = lse - high - middle
        return jnp.concatenate([high, middle, low, jnp.zeros((10, DH), F32)], axis=0).astype(BF16)

    def join(block):
        rows = block.astype(F32)
        return rows[0:2] + rows[2:4] + rows[4:6]

    def attend(h, k, offs):
        lanes = pl.ds(pl.multiple_of(h * DH, DH), DH)
        here = (ctx // stride_c(k)) % 4
        rows = [qbuf[h, (here + 4 - off) % 4].reshape(16, 16, DH).astype(F32) for off in offs]
        lse = []
        for s in range(2):
            q = jnp.concatenate([x[:, 8 * s : 8 * s + 8, :].reshape(DH, DH) for x in rows], axis=0).astype(BF16)
            edge = jnp.concatenate([bias[s]] * 2, axis=1)
            x0 = lax.dot_general(kbuf[s, :, lanes], q, NT, preferred_element_type=F32) * scale + edge[0:256]
            x1 = lax.dot_general(kdp[s, :, lanes], q, NT, preferred_element_type=F32) * scale + edge[256:272]
            peak = jnp.maximum(jnp.max(x0, axis=0, keepdims=True), jnp.max(x1, axis=0, keepdims=True))
            w0 = jnp.exp2(x0 - peak)
            w1 = jnp.exp2(x1 - peak)
            total = jnp.sum(w0, axis=0, keepdims=True) + jnp.sum(w1, axis=0, keepdims=True)
            numer = jnp.dot(vt[h, s], w0.astype(BF16), preferred_element_type=F32)
            numer += jnp.dot(vdt[h, s, :, 0:16], w1.astype(BF16), preferred_element_type=F32)
            part = (numer * (1.0 / total)).astype(BF16)
            lse.append(peak + jnp.log2(total))
            for i, off in enumerate(offs):
                s1[h, off, DH * s : DH * s + DH] = part[:, DH * i : DH * i + DH]
        for i, off in enumerate(offs):
            s1[h, off, 256:272] = split(jnp.concatenate([x[:, DH * i : DH * i + DH] for x in lse], axis=0))

    def merge(parts):
        peak = functools.reduce(jnp.maximum, parts)
        weights = [jnp.exp2(part - peak) for part in parts]
        total = functools.reduce(jnp.add, weights)
        inverse = 1.0 / total
        return [w * inverse for w in weights], peak + jnp.log2(total)

    def turned(factors):
        return jnp.concatenate(factors + [jnp.zeros((DH - 8, DH), F32)], axis=0).T

    def merge_first(h, k):
        for off in OFFS:
            first_back(h, k, off).wait_recv()
        parts = [s1.at[h, 0]] + [r1.at[h, off - 1] for off in (1, 2, 3)]
        factors, lse = merge([join(part[256:272]) for part in parts])
        tail = split(lse)
        for s in range(2):
            acc = parts[0][DH * s : DH * s + DH].astype(F32) * factors[0][s : s + 1]
            for i in (1, 2, 3):
                acc += parts[i][DH * s : DH * s + DH].astype(F32) * factors[i][s : s + 1]
            rows = acc.T.astype(BF16)
            for i in range(4):
                s2[h, i, 32 * s : 32 * s + 32] = rows[32 * i : 32 * i + 32]
        for i in range(4):
            s2[h, i, 64:80] = tail
        for off in OFFS:
            second_back(h, k, off).start()

    def merge_second(h, k):
        b = (ctx // stride_b(k)) % 4
        for off in OFFS:
            second_back(h, k, off).wait_recv()
        parts = [s2.at[h, b]] + [r2.at[h, off - 1] for off in (1, 2, 3)]
        factors, lse = merge([join(part[64:80]) for part in parts])
        tail = split(lse)
        factor[0] = turned(factors)
        columns = factor[0, pl.ds(pl.multiple_of(b * 32, 32), 32)]
        merged = []
        for s in range(2):
            acc = parts[0][32 * s : 32 * s + 32].astype(F32) * columns[:, s : s + 1]
            for i in (1, 2, 3):
                acc += parts[i][32 * s : 32 * s + 32].astype(F32) * columns[:, 2 * i + s : 2 * i + s + 1]
            merged.append(acc)
        for i in range(4):
            s3[h, i, 0:16] = jnp.concatenate([m[8 * i : 8 * i + 8] for m in merged], axis=0).astype(BF16)
            s3[h, i, 16:32] = tail
        for off in OFFS:
            third_back(h, k, off).start()

    def merge_third(h, k):
        a = (ctx // stride_a(k)) % 4
        b = (ctx // stride_b(k)) % 4
        for off in OFFS:
            third_back(h, k, off).wait_recv()
        parts = [s3.at[h, a]] + [r3.at[h, off - 1] for off in (1, 2, 3)]
        factors, _ = merge([join(part[16:32]) for part in parts])
        factor[1] = turned(factors)
        columns = factor[1, pl.ds(pl.multiple_of(b * 32 + a * 8, 8), 8)]
        acc = jnp.zeros((16, DH), F32)
        for i in range(4):
            column = jnp.concatenate([columns[:, 2 * i + s : 2 * i + s + 1] for s in range(2)], axis=0)
            acc += parts[i][0:16].astype(F32) * column
        attended[h] = acc

    @pl.loop(0, HEADS + LAG3)
    def _(t):
        @pl.when(t < HEADS)
        def _():
            h, k = head_of(t)
            a3(h, k, 1).wait_recv()
            attend(h, k, (0, 1))
            first_back(h, k, 1).start()
            a3(h, k, 3).wait_recv()
            a3(h, k, 2).wait_recv()
            attend(h, k, (3, 2))
            first_back(h, k, 3).start()
            first_back(h, k, 2).start()

        @pl.when((t >= LAG1) & (t < HEADS + LAG1))
        def _():
            merge_first(*head_of(t - LAG1))

        @pl.when((t >= LAG2) & (t < HEADS + LAG2))
        def _():
            merge_second(*head_of(t - LAG2))

        @pl.when(t >= LAG3)
        def _():
            merge_third(*head_of(t - LAG3))

    squares = attended[0] * attended[0]
    for h in range(1, HEADS):
        squares += attended[h] * attended[h]
    nsend[...] = squares

    def norm(off):
        return remote(nsend, nrecv.at[off - 1], ns.at[off - 1], nr.at[off - 1], (ctx, (tp + off) % 4))

    for off in (1, 2, 3):
        norm(off).start()

    for k in range(3):
        for off in OFFS:
            a1(k, off).wait_send()
            a2(k, off).wait_send()

    @pl.loop(0, HEADS)
    def _(t):
        h, k = head_of(t)
        for off in OFFS:
            a3(h, k, off).wait_send()
            first_back(h, k, off).wait_send()
            second_back(h, k, off).wait_send()
            third_back(h, k, off).wait_send()

    for off in (1, 2, 3):
        norm(off).wait()
    squares = squares + nrecv[0] + nrecv[1] + nrecv[2]
    mean = jnp.sum(squares, axis=1, keepdims=True) * (1.0 / (4 * HEADS * DH))
    inverse = lax.rsqrt(mean + 1e-06)
    for h in range(HEADS):
        y = attended[h] * inverse * gain_ref[h * DH : (h + 1) * DH].reshape(1, DH)
        for s in range(2):
            out_ref[s, :, h * DH : (h + 1) * DH] = y[8 * s : 8 * s + 8].astype(BF16)


def per_device(q_dec, k_dec, v_dec, ctx_k, ctx_v, lengths, gain):
    dma = pltpu.SemaphoreType.DMA
    hbm = pl.BlockSpec(memory_space=pltpu.HBM)
    scratch = [
        pltpu.VMEM((2, 8, HEADS * DH), BF16),
        pltpu.VMEM((2, 8, HEADS * DH), BF16),
        pltpu.VMEM((2, 8, HEADS * DH), BF16),
        pltpu.VMEM((2, 256, HEADS * DH), BF16),
        pltpu.VMEM((2, 256, HEADS * DH), BF16),
        pltpu.SMEM((2,), jnp.int32),
        pltpu.VMEM((HEADS * DH,), F32),
        pltpu.VMEM((HEADS, 4, 4, 4, 16, DH), BF16),
        pltpu.VMEM((HEADS, 4, 272, DH), BF16),
        pltpu.VMEM((HEADS, 3, 272, DH), BF16),
        pltpu.VMEM((HEADS, 4, 80, DH), BF16),
        pltpu.VMEM((HEADS, 3, 80, DH), BF16),
        pltpu.VMEM((HEADS, 4, 32, DH), BF16),
        pltpu.VMEM((HEADS, 3, 32, DH), BF16),
        pltpu.VMEM((2, DH, DH), F32),
        pltpu.VMEM((HEADS, 16, DH), F32),
        pltpu.VMEM((16, DH), F32),
        pltpu.VMEM((3, 16, DH), F32),
        pltpu.VMEM((HEADS, 2, DH, 256), BF16),
        pltpu.VMEM((2, 16, HEADS * DH), BF16),
        pltpu.VMEM((HEADS, 2, DH, DH), BF16),
        pltpu.VMEM((2, 272, DH), F32),
        dma((7,)),
        dma((3, 3)), dma((3, 3)), dma((3, 3)), dma((3, 3)),
        dma((HEADS, 3)), dma((HEADS, 3)), dma((HEADS, 3)), dma((HEADS, 3)),
        dma((HEADS, 3)), dma((HEADS, 3)), dma((HEADS, 3)), dma((HEADS, 3)),
        dma((3,)), dma((3,)),
    ]
    return pl.pallas_call(
        kernel,
        out_shape=jax.ShapeDtypeStruct(q_dec.shape, BF16),
        in_specs=[hbm] * 7,
        out_specs=pl.BlockSpec(memory_space=pltpu.VMEM),
        scratch_shapes=scratch,
        compiler_params=pltpu.CompilerParams(
            collective_id=0, has_side_effects=True, vmem_limit_bytes=62 << 20
        ),
        cost_estimate=pl.CostEstimate(flops=1_400_000_000, bytes_accessed=8_000_000, transcendentals=2_700_000),
        name="block_attention",
    )(q_dec, k_dec, v_dec, ctx_k, ctx_v, lengths, gain)


def solution(mesh):
    return jax.shard_map(
        per_device,
        mesh=mesh,
        in_specs=(
            P(None, "ctx", "tp"),
            P(None, "ctx", "tp"),
            P(None, "ctx", "tp"),
            P(None, "ctx", "tp"),
            P(None, "ctx", "tp"),
            P(),
            P("tp"),
        ),
        out_specs=P(None, "ctx", "tp"),
        check_vma=False,
    )
```

time: 1310 us -> 75 us (0.06)
  blocking collectives: 692 us -> 0 us
  waiting for transfers between devices: 506 us -> 0 us
  Pallas kernels: 0 us -> 73.4 us
  local copies, waits for them, and re-layouts: 57.9 us -> 1.4 us
  matrix products: 22.7 us -> 0 us
  between operations: 19.1 us -> 0.01 us
    unnamed x3 -> x0, waiting for transfers between devices: 431 us -> none
    unnamed x1 -> x0, blocking collectives: 329 us -> none
    pmax x1 -> x0, blocking collectives: 316 us -> none  [per_device(): lax.pmax(peak_all.astype(jnp.bfloat16), 'ctx').astype(peak_all.dtype)]
    all_gather x1 -> x0, waiting for transfers between devices: 75.1 us -> none  [per_device(): queries = lax.all_gather(q_dec, 'ctx', axis=1, tiled=True)]
    pallas_call x0 -> x1, Pallas kernels: none -> 73.4 us  [per_device(): pl.pallas_call(kernel, out_shape=jax.ShapeDtypeStruct(q_dec.shape, BF16),...]
    psum x1 -> x0, blocking collectives: 47.2 us -> none  [per_device(): total_sq = lax.psum(squares, 'tp')]
    dot_general x12 -> x0, matrix products: 22.7 us -> none  [the longest x4 11.4 us: absorb(): jnp.einsum('hqk,khd->hqd', block_weights.astype(jnp.bfloat16), block_valu...]
    slice x10 -> x0, local copies, waits for them, and re-layouts: 15.9 us -> none  [the longest x1 8.21 us: per_device(): query_rows = queries[sequence].reshape(total_rows, head_count, DH)]
  transfers between devices with their start and end apart: 2 -> 0, of which waited for: 2 -> 0; matrix products, arithmetic and copies ran while one was open for 1% -> 0% of each run, Pallas kernels for 0% -> 0%
where the time goes in v2:
time: 75 us; the launch traced here: 74.8 us
  Pallas kernels  73.4 us (98%)
  local copies, waits for them, and re-layouts  1.4 us (2%)
    pallas_call x1, Pallas kernels, per_device(): pl.pallas_call(kernel, out_shape=jax.ShapeDtypeStruct(q_dec.shape, BF16),...  73.4 us

profile of v2, /device:TPU:1, one launch (start us, length us, event | category | flops | bytes accessed | tf_op | source)
XLA Modules:
  0.0 74.8 jit_solution(16104143029106895653)
XLA Ops:
  0.0 73.4 %block_attention.1 = bf16[2,8,1280]{2,1,0:T(8,128)(2,1)} custom-call(bf16[2,8,1280]{2,1,0:T(8,128)(2,1)} %q_hbm.1, bf16[2,8,1280]{2,1,0:T(8,128)(2,1)} %kd_hbm.1, bf16[2,8,1280]{2,1,0:T(8,128)(2,1)} %vd_hbm.1, bf16[2,256,1280]{2,1,0:T(8,128)(2,1)} %ck_hbm.1, bf16[2,256,1280]{2,1,0:T(8,128)(2,1)} %cv_hbm.1, s32[2]{0:T(128)} %len_hbm.1, f32[1280]{0:T(1024)} %gain_hbm.1), custom_call_target="tpu_custom_call" | custom-call | flops 1400000000 | bytes 8000000 | tf_op jit(solution)/shard_map/block_attention/pallas_call | solution.py:340
  73.4 1.4 %copy.9 = bf16[2,8,1280]{2,1,0:T(8,128)(2,1)} copy(bf16[2,8,1280]{2,1,0:T(8,128)(2,1)} %block_attention.1) | data formatting | bytes 81920

commit v3 on v2

--- a/solution.py
+++ b/solution.py
@@ -18,19 +18,17 @@
 BF16 = jnp.bfloat16
 NT = (((1,), (1,)), ((), ()))
 OFFS = (1, 3, 2)
-LAG1, LAG2, LAG3 = 2, 4, 6
+LAG1, LAG2 = 4, 8
 
 
 def kernel(
     q_hbm, kd_hbm, vd_hbm, ck_hbm, cv_hbm, len_hbm, gain_hbm, out_ref,
     q_ref, kd_ref, vd_ref, kbuf, vbuf, len_ref, gain_ref,
-    qbuf, s1, r1, s2, r2, s3, r3, factor, attended, nsend, nrecv, vt, kdp, vdt, bias,
-    insem, a1s, a1r, a2s, a2r, a3s, a3r, r1s, r1r, r2s, r2r, r3s, r3r, ns, nr,
+    qbuf, s1, r1, s2, r2, s3, r3, attended, nsend, nrecv, vt, kdp, vdt, bias,
+    insem, g0s, g0r, g1s, g1r, g2s, g2r, g3s, g3r, r1s, r1r, r2s, r2r, r3s, r3r, ns, nr,
 ):
     ctx = lax.axis_index("ctx")
     tp = lax.axis_index("tp")
-    pos = {name: (ctx // STRIDE[name]) % 4 for name in "zyx"}
-
     loads = [
         pltpu.make_async_copy(src, dst, insem.at[i])
         for i, (src, dst) in enumerate((
@@ -52,12 +50,8 @@
 
     loads[0].wait()
     own = q_ref[...].astype(F32).reshape(16, HEADS * DH).astype(BF16)
-    place = []
-    for k, (first, count) in enumerate(CHUNKS):
-        a, b, c = (pos[name] for name in ORDER[k])
-        place.append((a, b, c))
-        for h in range(first, first + count):
-            qbuf[h, c, b, a] = own[:, h * DH : (h + 1) * DH]
+    for h in range(HEADS):
+        qbuf[h, 0, 0, 0] = own[:, h * DH : (h + 1) * DH]
 
     pl.semaphore_wait(barrier, 12)
 
@@ -66,21 +60,42 @@
             src_ref=src, dst_ref=dst, send_sem=send, recv_sem=recv, device_id=target, device_id_type=MESH
         )
 
-    def a1(k, off):
-        first, count = CHUNKS[k]
-        a, b, c = place[k]
-        block = qbuf.at[pl.ds(first, count), c, b, a]
-        return remote(block, block, a1s.at[k, off - 1], a1r.at[k, off - 1], along(STRIDE[ORDER[k][0]], off))
-
-    def a2(k, off):
-        first, count = CHUNKS[k]
-        a, b, c = place[k]
-        block = qbuf.at[pl.ds(first, count), c, b]
-        return remote(block, block, a2s.at[k, off - 1], a2r.at[k, off - 1], along(STRIDE[ORDER[k][1]], off))
+    def heads(k):
+        return pl.ds(CHUNKS[k][0], CHUNKS[k][1])
+
+    def own_block(k, axis, off):
+        spot = [0, 0, 0]
+        spot[2 - axis] = off
+        return remote(
+            qbuf.at[heads(k), 0, 0, 0], qbuf.at[heads(k), spot[0], spot[1], spot[2]],
+            g0s.at[k, axis, off - 1], g0r.at[k, axis, off - 1], along(STRIDE[ORDER[k][axis]], off),
+        )
+
+    def a_to_b(k, hop, off):
+        return remote(
+            qbuf.at[heads(k), 0, 0, hop], qbuf.at[heads(k), 0, off, hop],
+            g1s.at[k, hop - 1, off - 1], g1r.at[k, hop - 1, off - 1], along(STRIDE[ORDER[k][1]], off),
+        )
+
+    def a_to_c(k, off):
+        return remote(
+            qbuf.at[heads(k), 0, 0, pl.ds(1, 3)], qbuf.at[heads(k), off, 0, pl.ds(1, 3)],
+            g2s.at[k, 0, off - 1], g2r.at[k, 0, off - 1], along(STRIDE[ORDER[k][2]], off),
+        )
+
+    def b_to_c(k, off):
+        return remote(
+            qbuf.at[heads(k), 0, pl.ds(1, 3), 0], qbuf.at[heads(k), off, pl.ds(1, 3), 0],
+            g2s.at[k, 1, off - 1], g2r.at[k, 1, off - 1], along(STRIDE[ORDER[k][2]], off),
+        )
 
     for k in (2, 0, 1):
         for off in OFFS:
-            a1(k, off).start()
+            own_block(k, 0, off).start()
+    for axis in (1, 2):
+        for k in (2, 0, 1):
+            for off in OFFS:
+                own_block(k, axis, off).start()
 
     for load in loads[1:]:
         load.wait()
@@ -96,11 +111,18 @@
         for h in range(HEADS):
             vdt[h, s] = vpad[:, h * DH : (h + 1) * DH].T.astype(BF16)
 
+    for hop in OFFS:
+        for k in (2, 0, 1):
+            own_block(k, 0, hop).wait_recv()
+            for off in OFFS:
+                a_to_b(k, hop, off).start()
     for k in (2, 0, 1):
         for off in OFFS:
-            a1(k, off).wait_recv()
-        for off in OFFS:
-            a2(k, off).start()
+            a_to_c(k, off).start()
+        for off in OFFS:
+            own_block(k, 1, off).wait_recv()
+        for off in OFFS:
+            b_to_c(k, off).start()
 
     @pl.loop(0, HEADS)
     def _(h):
@@ -121,28 +143,34 @@
     def stride_c(k):
         return 1 + 3 * k + 9 * (k * (k - 1) // 2)
 
-    def a3(h, k, off):
-        block = qbuf.at[h, (ctx // stride_c(k)) % 4]
-        return remote(block, block, a3s.at[h, off - 1], a3r.at[h, off - 1], along(stride_c(k), off))
+    def ab_to_c(h, k, off):
+        return remote(
+            qbuf.at[h, 0, pl.ds(1, 3), pl.ds(1, 3)], qbuf.at[h, off, pl.ds(1, 3), pl.ds(1, 3)],
+            g3s.at[h, off - 1], g3r.at[h, off - 1], along(stride_c(k), off),
+        )
 
     def first_back(h, k, off):
         return remote(s1.at[h, off], r1.at[h, off - 1], r1s.at[h, off - 1], r1r.at[h, off - 1], along(stride_c(k), 4 - off))
 
     def second_back(h, k, off):
-        there = ((ctx // stride_b(k)) % 4 + off) % 4
-        return remote(s2.at[h, there], r2.at[h, off - 1], r2s.at[h, off - 1], r2r.at[h, off - 1], along(stride_b(k), off))
+        return remote(s2.at[h, off], r2.at[h, off - 1], r2s.at[h, off - 1], r2r.at[h, off - 1], along(stride_b(k), 4 - off))
 
     def third_back(h, k, off):
-        there = ((ctx // stride_a(k)) % 4 + off) % 4
-        return remote(s3.at[h, there], r3.at[h, off - 1], r3s.at[h, off - 1], r3r.at[h, off - 1], along(stride_a(k), off))
+        return remote(s3.at[h, off], r3.at[h, off - 1], r3s.at[h, off - 1], r3r.at[h, off - 1], along(stride_a(k), 4 - off))
 
     for k in (2, 0, 1):
         first, count = CHUNKS[k]
-        for off in OFFS:
-            a2(k, off).wait_recv()
+        for hop in OFFS:
+            for off in OFFS:
+                a_to_b(k, hop, off).wait_recv()
         for h in range(first, first + count):
             for off in OFFS:
-                a3(h, k, off).start()
+                ab_to_c(h, k, off).start()
+    for k in (2, 0, 1):
+        for off in OFFS:
+            own_block(k, 2, off).wait_recv()
+            a_to_c(k, off).wait_recv()
+            b_to_c(k, off).wait_recv()
 
     scale = math.log2(math.e) / math.sqrt(DH)
 
@@ -156,10 +184,9 @@
         rows = block.astype(F32)
         return rows[0:2] + rows[2:4] + rows[4:6]
 
-    def attend(h, k, offs):
+    def attend(h, offs):
         lanes = pl.ds(pl.multiple_of(h * DH, DH), DH)
-        here = (ctx // stride_c(k)) % 4
-        rows = [qbuf[h, (here + 4 - off) % 4].reshape(16, 16, DH).astype(F32) for off in offs]
+        rows = [qbuf[h, off].reshape(16, 16, DH).astype(F32) for off in offs]
         lse = []
         for s in range(2):
             q = jnp.concatenate([x[:, 8 * s : 8 * s + 8, :].reshape(DH, DH) for x in rows], axis=0).astype(BF16)
@@ -186,6 +213,9 @@
         inverse = 1.0 / total
         return [w * inverse for w in weights], peak + jnp.log2(total)
 
+    def shifted(rows, lanes):
+        return pltpu.roll(rows, DH - lanes, 1) if lanes else rows
+
     def turned(factors):
         return jnp.concatenate(factors + [jnp.zeros((DH - 8, DH), F32)], axis=0).T
 
@@ -208,14 +238,12 @@
             second_back(h, k, off).start()
 
     def merge_second(h, k):
-        b = (ctx // stride_b(k)) % 4
         for off in OFFS:
             second_back(h, k, off).wait_recv()
-        parts = [s2.at[h, b]] + [r2.at[h, off - 1] for off in (1, 2, 3)]
-        factors, lse = merge([join(part[64:80]) for part in parts])
+        parts = [s2.at[h, 0]] + [r2.at[h, off - 1] for off in (1, 2, 3)]
+        factors, lse = merge([shifted(join(part[64:80]), 32 * i) for i, part in enumerate(parts)])
         tail = split(lse)
-        factor[0] = turned(factors)
-        columns = factor[0, pl.ds(pl.multiple_of(b * 32, 32), 32)]
+        columns = turned(factors)[0:32]
         merged = []
         for s in range(2):
             acc = parts[0][32 * s : 32 * s + 32].astype(F32) * columns[:, s : s + 1]
@@ -229,45 +257,48 @@
             third_back(h, k, off).start()
 
     def merge_third(h, k):
-        a = (ctx // stride_a(k)) % 4
-        b = (ctx // stride_b(k)) % 4
         for off in OFFS:
             third_back(h, k, off).wait_recv()
-        parts = [s3.at[h, a]] + [r3.at[h, off - 1] for off in (1, 2, 3)]
-        factors, _ = merge([join(part[16:32]) for part in parts])
-        factor[1] = turned(factors)
-        columns = factor[1, pl.ds(pl.multiple_of(b * 32 + a * 8, 8), 8)]
+        parts = [s3.at[h, 0]] + [r3.at[h, off - 1] for off in (1, 2, 3)]
+        factors, _ = merge([shifted(join(part[16:32]), 8 * i) for i, part in enumerate(parts)])
+        columns = turned(factors)[0:8]
         acc = jnp.zeros((16, DH), F32)
         for i in range(4):
             column = jnp.concatenate([columns[:, 2 * i + s : 2 * i + s + 1] for s in range(2)], axis=0)
             acc += parts[i][0:16].astype(F32) * column
         attended[h] = acc
 
-    @pl.loop(0, HEADS + LAG3)
+    @pl.loop(0, HEADS)
     def _(t):
-        @pl.when(t < HEADS)
-        def _():
-            h, k = head_of(t)
-            a3(h, k, 1).wait_recv()
-            attend(h, k, (0, 1))
-            first_back(h, k, 1).start()
-            a3(h, k, 3).wait_recv()
-            a3(h, k, 2).wait_recv()
-            attend(h, k, (3, 2))
-            first_back(h, k, 3).start()
-            first_back(h, k, 2).start()
-
-        @pl.when((t >= LAG1) & (t < HEADS + LAG1))
+        h, k = head_of(t)
+        ab_to_c(h, k, 1).wait_recv()
+        attend(h, (0, 1))
+        first_back(h, k, 1).start()
+        ab_to_c(h, k, 3).wait_recv()
+        ab_to_c(h, k, 2).wait_recv()
+        attend(h, (3, 2))
+        first_back(h, k, 3).start()
+        first_back(h, k, 2).start()
+
+        @pl.when(t >= LAG1)
         def _():
             merge_first(*head_of(t - LAG1))
 
-        @pl.when((t >= LAG2) & (t < HEADS + LAG2))
+        @pl.when(t >= LAG2)
         def _():
             merge_second(*head_of(t - LAG2))
 
-        @pl.when(t >= LAG3)
-        def _():
-            merge_third(*head_of(t - LAG3))
+    @pl.loop(HEADS - LAG1, HEADS)
+    def _(t):
+        merge_first(*head_of(t))
+
+    @pl.loop(HEADS - LAG2, HEADS)
+    def _(t):
+        merge_second(*head_of(t))
+
+    @pl.loop(0, HEADS)
+    def _(t):
+        merge_third(*head_of(t))
 
     squares = attended[0] * attended[0]
     for h in range(1, HEADS):
@@ -282,14 +313,18 @@
 
     for k in range(3):
         for off in OFFS:
-            a1(k, off).wait_send()
-            a2(k, off).wait_send()
+            for axis in range(3):
+                own_block(k, axis, off).wait_send()
+            for hop in OFFS:
+                a_to_b(k, hop, off).wait_send()
+            a_to_c(k, off).wait_send()
+            b_to_c(k, off).wait_send()
 
     @pl.loop(0, HEADS)
     def _(t):
         h, k = head_of(t)
         for off in OFFS:
-            a3(h, k, off).wait_send()
+            ab_to_c(h, k, off).wait_send()
             first_back(h, k, off).wait_send()
             second_back(h, k, off).wait_send()
             third_back(h, k, off).wait_send()
@@ -323,7 +358,6 @@
         pltpu.VMEM((HEADS, 3, 80, DH), BF16),
         pltpu.VMEM((HEADS, 4, 32, DH), BF16),
         pltpu.VMEM((HEADS, 3, 32, DH), BF16),
-        pltpu.VMEM((2, DH, DH), F32),
         pltpu.VMEM((HEADS, 16, DH), F32),
         pltpu.VMEM((16, DH), F32),
         pltpu.VMEM((3, 16, DH), F32),
@@ -332,7 +366,7 @@
         pltpu.VMEM((HEADS, 2, DH, DH), BF16),
         pltpu.VMEM((2, 272, DH), F32),
         dma((7,)),
-        dma((3, 3)), dma((3, 3)), dma((3, 3)), dma((3, 3)),
+        dma((3, 3, 3)), dma((3, 3, 3)), dma((3, 3, 3)), dma((3, 3, 3)), dma((3, 2, 3)), dma((3, 2, 3)),
         dma((HEADS, 3)), dma((HEADS, 3)), dma((HEADS, 3)), dma((HEADS, 3)),
         dma((HEADS, 3)), dma((HEADS, 3)), dma((HEADS, 3)), dma((HEADS, 3)),
         dma((3,)), dma((3,)),

time: 75 us -> 65.4 us (0.87)
  Pallas kernels: 73.4 us -> 63.8 us
    pallas_call x1, Pallas kernels: 73.4 us -> 63.8 us  [per_device(): pl.pallas_call(kernel, out_shape=jax.ShapeDtypeStruct(q_dec.shape, BF16),...]
where the time goes in v3:
time: 65.4 us; the launch traced here: 65.2 us
  Pallas kernels  63.8 us (98%)
  local copies, waits for them, and re-layouts  1.4 us (2%)
    pallas_call x1, Pallas kernels, per_device(): pl.pallas_call(kernel, out_shape=jax.ShapeDtypeStruct(q_dec.shape, BF16),...  63.8 us
    unnamed x1, local copies, waits for them, and re-layouts  1.4 us

profile of v3, /device:TPU:1, one launch (start us, length us, event | category | flops | bytes accessed | tf_op | source)
XLA Modules:
  0.0 65.2 jit_solution(16617626769397685071)
XLA Ops:
  0.0 63.8 %block_attention.1 = bf16[2,8,1280]{2,1,0:T(8,128)(2,1)} custom-call(bf16[2,8,1280]{2,1,0:T(8,128)(2,1)} %q_hbm.1, bf16[2,8,1280]{2,1,0:T(8,128)(2,1)} %kd_hbm.1, bf16[2,8,1280]{2,1,0:T(8,128)(2,1)} %vd_hbm.1, bf16[2,256,1280]{2,1,0:T(8,128)(2,1)} %ck_hbm.1, bf16[2,256,1280]{2,1,0:T(8,128)(2,1)} %cv_hbm.1, s32[2]{0:T(128)} %len_hbm.1, f32[1280]{0:T(1024)} %gain_hbm.1), custom_call_target="tpu_custom_call" | custom-call | flops 1400000000 | bytes 8000000 | tf_op jit(solution)/shard_map/block_attention/pallas_call | solution.py:374
  63.8 1.4 %copy.9 = bf16[2,8,1280]{2,1,0:T(8,128)(2,1)} copy(bf16[2,8,1280]{2,1,0:T(8,128)(2,1)} %block_attention.1) | data formatting | bytes 81920

commit v4 on v3

--- a/solution.py
+++ b/solution.py
@@ -18,7 +18,8 @@
 BF16 = jnp.bfloat16
 NT = (((1,), (1,)), ((), ()))
 OFFS = (1, 3, 2)
-LAG1, LAG2 = 4, 8
+STEPS, LAG1 = 5, 4
+ATTEND = (0, 4, 3, 2, 1)
 
 
 def kernel(
@@ -35,9 +36,6 @@
             (q_hbm, q_ref), (kd_hbm, kd_ref), (vd_hbm, vd_ref), (ck_hbm, kbuf), (cv_hbm, vbuf), (len_hbm, len_ref), (gain_hbm, gain_ref),
         ))
     ]
-    for load in loads:
-        load.start()
-
     def along(stride, off):
         here = (ctx // stride) % 4
         return (ctx + ((here + off) % 4 - here) * stride, tp)
@@ -47,6 +45,9 @@
         for name in "zyx":
             pl.semaphore_signal(barrier, inc=1, device_id=along(STRIDE[name], off), device_id_type=MESH)
         pl.semaphore_signal(barrier, inc=1, device_id=(ctx, (tp + off) % 4), device_id_type=MESH)
+
+    for load in loads:
+        load.start()
 
     loads[0].wait()
     own = q_ref[...].astype(F32).reshape(16, HEADS * DH).astype(BF16)
@@ -88,6 +89,25 @@
             qbuf.at[heads(k), 0, pl.ds(1, 3), 0], qbuf.at[heads(k), off, pl.ds(1, 3), 0],
             g2s.at[k, 1, off - 1], g2r.at[k, 1, off - 1], along(STRIDE[ORDER[k][2]], off),
         )
+
+    def ab_to_c(h, k, off):
+        return remote(
+            qbuf.at[h, 0, pl.ds(1, 3), pl.ds(1, 3)], qbuf.at[h, off, pl.ds(1, 3), pl.ds(1, 3)],
+            g3s.at[h, off - 1], g3r.at[h, off - 1], along(stride_c(k), off),
+        )
+
+    def pair(n):
+        z = n // 4
+        return ((8 * z + (1 - z) * n, 2 * z), (9 * z + (1 - z) * (4 + n), 1 + z))
+
+    def stride_a(k):
+        return 16 - 15 * (k * (k - 1) // 2)
+
+    def stride_b(k):
+        return 4 - 3 * (k * (2 - k))
+
+    def stride_c(k):
+        return 1 + 3 * k + 9 * (k * (k - 1) // 2)
 
     for k in (2, 0, 1):
         for off in OFFS:
@@ -123,6 +143,14 @@
             own_block(k, 1, off).wait_recv()
         for off in OFFS:
             b_to_c(k, off).start()
+    for k in (2, 0, 1):
+        for hop in OFFS:
+            for off in OFFS:
+                a_to_b(k, hop, off).wait_recv()
+    for n in ATTEND:
+        for h, k in pair(n):
+            for off in OFFS:
+                ab_to_c(h, k, off).start()
 
     @pl.loop(0, HEADS)
     def _(h):
@@ -130,25 +158,6 @@
         for s in range(2):
             vt[h, s] = vbuf[s, :, lanes].astype(F32).T.astype(BF16)
 
-    def head_of(t):
-        k = (t % 5) % 3
-        return 4 * k + (t // 5) * (2 - k // 2) + (t % 5) // 3, k
-
-    def stride_a(k):
-        return 16 - 15 * (k * (k - 1) // 2)
-
-    def stride_b(k):
-        return 4 - 3 * (k * (2 - k))
-
-    def stride_c(k):
-        return 1 + 3 * k + 9 * (k * (k - 1) // 2)
-
-    def ab_to_c(h, k, off):
-        return remote(
-            qbuf.at[h, 0, pl.ds(1, 3), pl.ds(1, 3)], qbuf.at[h, off, pl.ds(1, 3), pl.ds(1, 3)],
-            g3s.at[h, off - 1], g3r.at[h, off - 1], along(stride_c(k), off),
-        )
-
     def first_back(h, k, off):
         return remote(s1.at[h, off], r1.at[h, off - 1], r1s.at[h, off - 1], r1r.at[h, off - 1], along(stride_c(k), 4 - off))
 
@@ -157,20 +166,6 @@
 
     def third_back(h, k, off):
         return remote(s3.at[h, off], r3.at[h, off - 1], r3s.at[h, off - 1], r3r.at[h, off - 1], along(stride_a(k), 4 - off))
-
-    for k in (2, 0, 1):
-        first, count = CHUNKS[k]
-        for hop in OFFS:
-            for off in OFFS:
-                a_to_b(k, hop, off).wait_recv()
-        for h in range(first, first + count):
-            for off in OFFS:
-                ab_to_c(h, k, off).start()
-    for k in (2, 0, 1):
-        for off in OFFS:
-            own_block(k, 2, off).wait_recv()
-            a_to_c(k, off).wait_recv()
-            b_to_c(k, off).wait_recv()
 
     scale = math.log2(math.e) / math.sqrt(DH)
 
@@ -190,7 +185,7 @@
         lse = []
         for s in range(2):
             q = jnp.concatenate([x[:, 8 * s : 8 * s + 8, :].reshape(DH, DH) for x in rows], axis=0).astype(BF16)
-            edge = jnp.concatenate([bias[s]] * 2, axis=1)
+            edge = jnp.concatenate([bias[s]] * len(offs), axis=1)
             x0 = lax.dot_general(kbuf[s, :, lanes], q, NT, preferred_element_type=F32) * scale + edge[0:256]
             x1 = lax.dot_general(kdp[s, :, lanes], q, NT, preferred_element_type=F32) * scale + edge[256:272]
             peak = jnp.maximum(jnp.max(x0, axis=0, keepdims=True), jnp.max(x1, axis=0, keepdims=True))
@@ -219,86 +214,116 @@
     def turned(factors):
         return jnp.concatenate(factors + [jnp.zeros((DH - 8, DH), F32)], axis=0).T
 
-    def merge_first(h, k):
-        for off in OFFS:
-            first_back(h, k, off).wait_recv()
-        parts = [s1.at[h, 0]] + [r1.at[h, off - 1] for off in (1, 2, 3)]
-        factors, lse = merge([join(part[256:272]) for part in parts])
-        tail = split(lse)
-        for s in range(2):
-            acc = parts[0][DH * s : DH * s + DH].astype(F32) * factors[0][s : s + 1]
-            for i in (1, 2, 3):
-                acc += parts[i][DH * s : DH * s + DH].astype(F32) * factors[i][s : s + 1]
-            rows = acc.T.astype(BF16)
+    def merge_first(t):
+        for h, k in pair(t):
+            for off in OFFS:
+                first_back(h, k, off).wait_recv()
+        results = []
+        for h, k in pair(t):
+            parts = [s1.at[h, 0]] + [r1.at[h, off - 1] for off in (1, 2, 3)]
+            factors, lse = merge([join(part[256:272]) for part in parts])
+            rows = []
+            for s in range(2):
+                acc = parts[0][DH * s : DH * s + DH].astype(F32) * factors[0][s : s + 1]
+                for i in (1, 2, 3):
+                    acc += parts[i][DH * s : DH * s + DH].astype(F32) * factors[i][s : s + 1]
+                rows.append(acc.T.astype(BF16))
+            results.append((h, rows, split(lse)))
+        for h, rows, tail in results:
             for i in range(4):
-                s2[h, i, 32 * s : 32 * s + 32] = rows[32 * i : 32 * i + 32]
-        for i in range(4):
-            s2[h, i, 64:80] = tail
-        for off in OFFS:
-            second_back(h, k, off).start()
-
-    def merge_second(h, k):
-        for off in OFFS:
-            second_back(h, k, off).wait_recv()
-        parts = [s2.at[h, 0]] + [r2.at[h, off - 1] for off in (1, 2, 3)]
-        factors, lse = merge([shifted(join(part[64:80]), 32 * i) for i, part in enumerate(parts)])
-        tail = split(lse)
-        columns = turned(factors)[0:32]
-        merged = []
-        for s in range(2):
-            acc = parts[0][32 * s : 32 * s + 32].astype(F32) * columns[:, s : s + 1]
-            for i in (1, 2, 3):
-                acc += parts[i][32 * s : 32 * s + 32].astype(F32) * columns[:, 2 * i + s : 2 * i + s + 1]
-            merged.append(acc)
-        for i in range(4):
-            s3[h, i, 0:16] = jnp.concatenate([m[8 * i : 8 * i + 8] for m in merged], axis=0).astype(BF16)
-            s3[h, i, 16:32] = tail
-        for off in OFFS:
-            third_back(h, k, off).start()
-
-    def merge_third(h, k):
-        for off in OFFS:
-            third_back(h, k, off).wait_recv()
-        parts = [s3.at[h, 0]] + [r3.at[h, off - 1] for off in (1, 2, 3)]
-        factors, _ = merge([shifted(join(part[16:32]), 8 * i) for i, part in enumerate(parts)])
-        columns = turned(factors)[0:8]
-        acc = jnp.zeros((16, DH), F32)
-        for i in range(4):
-            column = jnp.concatenate([columns[:, 2 * i + s : 2 * i + s + 1] for s in range(2)], axis=0)
-            acc += parts[i][0:16].astype(F32) * column
-        attended[h] = acc
-
-    @pl.loop(0, HEADS)
+                for s in range(2):
+                    s2[h, i, 32 * s : 32 * s + 32] = rows[s][32 * i : 32 * i + 32]
+                s2[h, i, 64:80] = tail
+        for h, k in pair(t):
+            for off in OFFS:
+                second_back(h, k, off).start()
+
+    def merge_second(t):
+        for h, k in pair(t):
+            for off in OFFS:
+                second_back(h, k, off).wait_recv()
+        results = []
+        for h, k in pair(t):
+            parts = [s2.at[h, 0]] + [r2.at[h, off - 1] for off in (1, 2, 3)]
+            factors, lse = merge([shifted(join(part[64:80]), 32 * i) for i, part in enumerate(parts)])
+            columns = turned(factors)[0:32]
+            merged = []
+            for s in range(2):
+                acc = parts[0][32 * s : 32 * s + 32].astype(F32) * columns[:, s : s + 1]
+                for i in (1, 2, 3):
+                    acc += parts[i][32 * s : 32 * s + 32].astype(F32) * columns[:, 2 * i + s : 2 * i + s + 1]
+                merged.append(acc)
+            results.append((h, merged, split(lse)))
+        for h, merged, tail in results:
+            for i in range(4):
+                s3[h, i, 0:16] = jnp.concatenate([m[8 * i : 8 * i + 8] for m in merged], axis=0).astype(BF16)
+                s3[h, i, 16:32] = tail
+        for h, k in pair(t):
+            for off in OFFS:
+                third_back(h, k, off).start()
+
+    def merge_third(t):
+        for h, k in pair(t):
+            for off in OFFS:
+                third_back(h, k, off).wait_recv()
+        results = []
+        for h, k in pair(t):
+            parts = [s3.at[h, 0]] + [r3.at[h, off - 1] for off in (1, 2, 3)]
+            factors, _ = merge([shifted(join(part[16:32]), 8 * i) for i, part in enumerate(parts)])
+            columns = turned(factors)[0:8]
+            acc = jnp.zeros((16, DH), F32)
+            for i in range(4):
+                column = jnp.concatenate([columns[:, 2 * i + s : 2 * i + s + 1] for s in range(2)], axis=0)
+                acc += parts[i][0:16].astype(F32) * column
+            results.append((h, acc))
+        for h, acc in results:
+            attended[h] = acc
+
+    @pl.loop(0, STEPS)
     def _(t):
-        h, k = head_of(t)
-        ab_to_c(h, k, 1).wait_recv()
-        attend(h, (0, 1))
-        first_back(h, k, 1).start()
-        ab_to_c(h, k, 3).wait_recv()
-        ab_to_c(h, k, 2).wait_recv()
-        attend(h, (3, 2))
-        first_back(h, k, 3).start()
-        first_back(h, k, 2).start()
+        for h, _ in pair(t):
+            attend(h, (0,))
+
+    for k in (2, 0, 1):
+        for off in OFFS:
+            own_block(k, 2, off).wait_recv()
+            a_to_c(k, off).wait_recv()
+            b_to_c(k, off).wait_recv()
+
+    def merged(i):
+        return ((i + 3) // 4) * (4 - i) + 4 * (i // 4)
+
+    @pl.loop(0, STEPS)
+    def _(t):
+        for h, k in pair((4 * t) % 5):
+            for off in OFFS:
+                ab_to_c(h, k, off).wait_recv()
+        for h, k in pair((4 * t) % 5):
+            attend(h, (1, 3, 2))
+            for off in OFFS:
+                first_back(h, k, off).start()
 
         @pl.when(t >= LAG1)
         def _():
-            merge_first(*head_of(t - LAG1))
-
-        @pl.when(t >= LAG2)
-        def _():
-            merge_second(*head_of(t - LAG2))
-
-    @pl.loop(HEADS - LAG1, HEADS)
-    def _(t):
-        merge_first(*head_of(t))
-
-    @pl.loop(HEADS - LAG2, HEADS)
-    def _(t):
-        merge_second(*head_of(t))
-
-    @pl.loop(0, HEADS)
-    def _(t):
-        merge_third(*head_of(t))
+            merge_first(merged(t - LAG1))
+
+    merge_first(merged(STEPS - LAG1))
+
+    @pl.loop(0, STEPS - LAG1)
+    def _(i):
+        merge_second(merged(i))
+
+    @pl.loop(STEPS - LAG1 + 1, STEPS)
+    def _(i):
+        merge_first(merged(i))
+
+    @pl.loop(STEPS - LAG1, STEPS)
+    def _(i):
+        merge_second(merged(i))
+
+    @pl.loop(0, STEPS)
+    def _(i):
+        merge_third(merged(i))
 
     squares = attended[0] * attended[0]
     for h in range(1, HEADS):
@@ -320,14 +345,14 @@
             a_to_c(k, off).wait_send()
             b_to_c(k, off).wait_send()
 
-    @pl.loop(0, HEADS)
+    @pl.loop(0, STEPS)
     def _(t):
-        h, k = head_of(t)
-        for off in OFFS:
-            ab_to_c(h, k, off).wait_send()
-            first_back(h, k, off).wait_send()
-            second_back(h, k, off).wait_send()
-            third_back(h, k, off).wait_send()
+        for h, k in pair(t):
+            for off in OFFS:
+                ab_to_c(h, k, off).wait_send()
+                first_back(h, k, off).wait_send()
+                second_back(h, k, off).wait_send()
+                third_back(h, k, off).wait_send()
 
     for off in (1, 2, 3):
         norm(off).wait()

time: 65.4 us -> 63.9 us (0.977)
  Pallas kernels: 63.8 us -> 62.3 us
    pallas_call x1, Pallas kernels: 63.8 us -> 62.3 us  [per_device(): pl.pallas_call(kernel, out_shape=jax.ShapeDtypeStruct(q_dec.shape, BF16),...]
where the time goes in v4:
time: 63.9 us; the launch traced here: 63.7 us
  Pallas kernels  62.3 us (97%)
  local copies, waits for them, and re-layouts  1.4 us (2%)
    pallas_call x1, Pallas kernels, per_device(): pl.pallas_call(kernel, out_shape=jax.ShapeDtypeStruct(q_dec.shape, BF16),...  62.3 us
    unnamed x1, local copies, waits for them, and re-layouts  1.4 us

profile of v4, /device:TPU:1, one launch (start us, length us, event | category | flops | bytes accessed | tf_op | source)
XLA Modules:
  0.0 63.7 jit_solution(17634111842923213182)
XLA Ops:
  0.0 62.3 %block_attention.1 = bf16[2,8,1280]{2,1,0:T(8,128)(2,1)} custom-call(bf16[2,8,1280]{2,1,0:T(8,128)(2,1)} %q_hbm.1, bf16[2,8,1280]{2,1,0:T(8,128)(2,1)} %kd_hbm.1, bf16[2,8,1280]{2,1,0:T(8,128)(2,1)} %vd_hbm.1, bf16[2,256,1280]{2,1,0:T(8,128)(2,1)} %ck_hbm.1, bf16[2,256,1280]{2,1,0:T(8,128)(2,1)} %cv_hbm.1, s32[2]{0:T(128)} %len_hbm.1, f32[1280]{0:T(1024)} %gain_hbm.1), custom_call_target="tpu_custom_call" | custom-call | flops 1400000000 | bytes 8000000 | tf_op jit(solution)/shard_map/block_attention/pallas_call | solution.py:399
  62.3 1.4 %copy.9 = bf16[2,8,1280]{2,1,0:T(8,128)(2,1)} copy(bf16[2,8,1280]{2,1,0:T(8,128)(2,1)} %block_attention.1) | data formatting | bytes 81920

commit v5 on v4

--- a/solution.py
+++ b/solution.py
@@ -18,14 +18,15 @@
 BF16 = jnp.bfloat16
 NT = (((1,), (1,)), ((), ()))
 OFFS = (1, 3, 2)
-STEPS, LAG1 = 5, 4
+FAR = (2, 1, 3)
+STEPS = 5
 ATTEND = (0, 4, 3, 2, 1)
 
 
 def kernel(
     q_hbm, kd_hbm, vd_hbm, ck_hbm, cv_hbm, len_hbm, gain_hbm, out_ref,
     q_ref, kd_ref, vd_ref, kbuf, vbuf, len_ref, gain_ref,
-    qbuf, s1, r1, s2, r2, s3, r3, attended, nsend, nrecv, vt, kdp, vdt, bias,
+    qbuf, s1, r1, s2, r2, s3, r3, attended, nsend, nrecv, vt, kdp, vdb, bias,
     insem, g0s, g0r, g1s, g1r, g2s, g2r, g3s, g3r, r1s, r1r, r2s, r2r, r3s, r3r, ns, nr,
 ):
     ctx = lax.axis_index("ctx")
@@ -41,7 +42,7 @@
         return (ctx + ((here + off) % 4 - here) * stride, tp)
 
     barrier = pltpu.get_barrier_semaphore()
-    for off in (1, 2, 3):
+    for off in (2, 1, 3):
         for name in "zyx":
             pl.semaphore_signal(barrier, inc=1, device_id=along(STRIDE[name], off), device_id_type=MESH)
         pl.semaphore_signal(barrier, inc=1, device_id=(ctx, (tp + off) % 4), device_id_type=MESH)
@@ -64,6 +65,13 @@
     def heads(k):
         return pl.ds(CHUNKS[k][0], CHUNKS[k][1])
 
+    def own_z(off):
+        both = pl.ds(0, 8)
+        return remote(
+            qbuf.at[both, 0, 0, 0], qbuf.at[both, 0, 0, off],
+            g0s.at[0, 0, off - 1], g0r.at[0, 0, off - 1], along(STRIDE["z"], off),
+        )
+
     def own_block(k, axis, off):
         spot = [0, 0, 0]
         spot[2 - axis] = off
@@ -109,12 +117,13 @@
     def stride_c(k):
         return 1 + 3 * k + 9 * (k * (k - 1) // 2)
 
-    for k in (2, 0, 1):
-        for off in OFFS:
-            own_block(k, 0, off).start()
+    for off in FAR:
+        own_z(off).start()
+    for off in FAR:
+        own_block(2, 0, off).start()
     for axis in (1, 2):
         for k in (2, 0, 1):
-            for off in OFFS:
+            for off in FAR:
                 own_block(k, axis, off).start()
 
     for load in loads[1:]:
@@ -129,19 +138,24 @@
         kdp[s] = jnp.concatenate([kd_ref[s].astype(F32), pad], axis=0).astype(BF16)
         vpad = jnp.concatenate([vd_ref[s].astype(F32), jnp.zeros((DH - 8, HEADS * DH), F32)], axis=0)
         for h in range(HEADS):
-            vdt[h, s] = vpad[:, h * DH : (h + 1) * DH].T.astype(BF16)
+            turned_values = vpad[:, h * DH : (h + 1) * DH].T
+            for j in range(8):
+                vdb[h, s, j] = jnp.broadcast_to(turned_values[:, j : j + 1], (DH, DH))
 
     for hop in OFFS:
         for k in (2, 0, 1):
-            own_block(k, 0, hop).wait_recv()
-            for off in OFFS:
+            if k == 0:
+                own_z(hop).wait_recv()
+            if k == 2:
+                own_block(k, 0, hop).wait_recv()
+            for off in FAR:
                 a_to_b(k, hop, off).start()
     for k in (2, 0, 1):
-        for off in OFFS:
+        for off in FAR:
             a_to_c(k, off).start()
         for off in OFFS:
             own_block(k, 1, off).wait_recv()
-        for off in OFFS:
+        for off in FAR:
             b_to_c(k, off).start()
     for k in (2, 0, 1):
         for hop in OFFS:
@@ -149,7 +163,7 @@
                 a_to_b(k, hop, off).wait_recv()
     for n in ATTEND:
         for h, k in pair(n):
-            for off in OFFS:
+            for off in FAR:
                 ab_to_c(h, k, off).start()
 
     @pl.loop(0, HEADS)
@@ -193,7 +207,14 @@
             w1 = jnp.exp2(x1 - peak)
             total = jnp.sum(w0, axis=0, keepdims=True) + jnp.sum(w1, axis=0, keepdims=True)
             numer = jnp.dot(vt[h, s], w0.astype(BF16), preferred_element_type=F32)
-            numer += jnp.dot(vdt[h, s, :, 0:16], w1.astype(BF16), preferred_element_type=F32)
+            w1 = w1.astype(BF16).astype(F32)
+            block = []
+            for i in range(len(offs)):
+                own_part = vdb[h, s, 0] * w1[0:1, DH * i : DH * i + DH]
+                for j in range(1, 8):
+                    own_part += vdb[h, s, j] * w1[j : j + 1, DH * i : DH * i + DH]
+                block.append(own_part)
+            numer += jnp.concatenate(block, axis=1)
             part = (numer * (1.0 / total)).astype(BF16)
             lse.append(peak + jnp.log2(total))
             for i, off in enumerate(offs):
@@ -214,12 +235,13 @@
     def turned(factors):
         return jnp.concatenate(factors + [jnp.zeros((DH - 8, DH), F32)], axis=0).T
 
-    def merge_first(t):
-        for h, k in pair(t):
+    def merge_first(*pairs):
+        todo = [entry for n in pairs for entry in pair(n)]
+        for h, k in todo:
             for off in OFFS:
                 first_back(h, k, off).wait_recv()
         results = []
-        for h, k in pair(t):
+        for h, k in todo:
             parts = [s1.at[h, 0]] + [r1.at[h, off - 1] for off in (1, 2, 3)]
             factors, lse = merge([join(part[256:272]) for part in parts])
             rows = []
@@ -234,16 +256,17 @@
                 for s in range(2):
                     s2[h, i, 32 * s : 32 * s + 32] = rows[s][32 * i : 32 * i + 32]
                 s2[h, i, 64:80] = tail
-        for h, k in pair(t):
-            for off in OFFS:
+        for h, k in todo:
+            for off in FAR:
                 second_back(h, k, off).start()
 
-    def merge_second(t):
-        for h, k in pair(t):
+    def merge_second(*pairs):
+        todo = [entry for n in pairs for entry in pair(n)]
+        for h, k in todo:
             for off in OFFS:
                 second_back(h, k, off).wait_recv()
         results = []
-        for h, k in pair(t):
+        for h, k in todo:
             parts = [s2.at[h, 0]] + [r2.at[h, off - 1] for off in (1, 2, 3)]
             factors, lse = merge([shifted(join(part[64:80]), 32 * i) for i, part in enumerate(parts)])
             columns = turned(factors)[0:32]
@@ -258,16 +281,17 @@
             for i in range(4):
                 s3[h, i, 0:16] = jnp.concatenate([m[8 * i : 8 * i + 8] for m in merged], axis=0).astype(BF16)
                 s3[h, i, 16:32] = tail
-        for h, k in pair(t):
-            for off in OFFS:
+        for h, k in todo:
+            for off in FAR:
                 third_back(h, k, off).start()
 
-    def merge_third(t):
-        for h, k in pair(t):
+    def merge_third(*pairs):
+        todo = [entry for n in pairs for entry in pair(n)]
+        for h, k in todo:
             for off in OFFS:
                 third_back(h, k, off).wait_recv()
         results = []
-        for h, k in pair(t):
+        for h, k in todo:
             parts = [s3.at[h, 0]] + [r3.at[h, off - 1] for off in (1, 2, 3)]
             factors, _ = merge([shifted(join(part[16:32]), 8 * i) for i, part in enumerate(parts)])
             columns = turned(factors)[0:8]
@@ -290,9 +314,6 @@
             a_to_c(k, off).wait_recv()
             b_to_c(k, off).wait_recv()
 
-    def merged(i):
-        return ((i + 3) // 4) * (4 - i) + 4 * (i // 4)
-
     @pl.loop(0, STEPS)
     def _(t):
         for h, k in pair((4 * t) % 5):
@@ -300,30 +321,14 @@
                 ab_to_c(h, k, off).wait_recv()
         for h, k in pair((4 * t) % 5):
             attend(h, (1, 3, 2))
-            for off in OFFS:
+            for off in FAR:
                 first_back(h, k, off).start()
 
-        @pl.when(t >= LAG1)
-        def _():
-            merge_first(merged(t - LAG1))
-
-    merge_first(merged(STEPS - LAG1))
-
-    @pl.loop(0, STEPS - LAG1)
-    def _(i):
-        merge_second(merged(i))
-
-    @pl.loop(STEPS - LAG1 + 1, STEPS)
-    def _(i):
-        merge_first(merged(i))
-
-    @pl.loop(STEPS - LAG1, STEPS)
-    def _(i):
-        merge_second(merged(i))
-
-    @pl.loop(0, STEPS)
-    def _(i):
-        merge_third(merged(i))
+    merge_first(0, 3, 2)
+    merge_first(1, 4)
+    merge_second(0, 3, 2)
+    merge_second(1, 4)
+    merge_third(0, 3, 2, 1, 4)
 
     squares = attended[0] * attended[0]
     for h in range(1, HEADS):
@@ -339,7 +344,10 @@
     for k in range(3):
         for off in OFFS:
             for axis in range(3):
-                own_block(k, axis, off).wait_send()
+                if axis > 0 or k == 2:
+                    own_block(k, axis, off).wait_send()
+            if k == 0:
+                own_z(off).wait_send()
             for hop in OFFS:
                 a_to_b(k, hop, off).wait_send()
             a_to_c(k, off).wait_send()
@@ -388,7 +396,7 @@
         pltpu.VMEM((3, 16, DH), F32),
         pltpu.VMEM((HEADS, 2, DH, 256), BF16),
         pltpu.VMEM((2, 16, HEADS * DH), BF16),
-        pltpu.VMEM((HEADS, 2, DH, DH), BF16),
+        pltpu.VMEM((HEADS, 2, 8, DH, DH), F32),
         pltpu.VMEM((2, 272, DH), F32),
         dma((7,)),
         dma((3, 3, 3)), dma((3, 3, 3)), dma((3, 3, 3)), dma((3, 3, 3)), dma((3, 2, 3)), dma((3, 2, 3)),

time: 63.9 us -> 62.3 us (0.975)
  Pallas kernels: 62.3 us -> 60.7 us
    pallas_call x1, Pallas kernels: 62.3 us -> 60.7 us  [per_device(): pl.pallas_call(kernel, out_shape=jax.ShapeDtypeStruct(q_dec.shape, BF16),...]
where the time goes in v5:
time: 62.3 us; the launch traced here: 62.1 us
  Pallas kernels  60.7 us (97%)
  local copies, waits for them, and re-layouts  1.4 us (2%)
    pallas_call x1, Pallas kernels, per_device(): pl.pallas_call(kernel, out_shape=jax.ShapeDtypeStruct(q_dec.shape, BF16),...  60.7 us
    unnamed x1, local copies, waits for them, and re-layouts  1.4 us

profile of v5, /device:TPU:1, one launch (start us, length us, event | category | flops | bytes accessed | tf_op | source)
XLA Modules:
  0.0 62.1 jit_solution(11168109047861970523)
XLA Ops:
  0.0 60.7 %block_attention.1 = bf16[2,8,1280]{2,1,0:T(8,128)(2,1)} custom-call(bf16[2,8,1280]{2,1,0:T(8,128)(2,1)} %q_hbm.1, bf16[2,8,1280]{2,1,0:T(8,128)(2,1)} %kd_hbm.1, bf16[2,8,1280]{2,1,0:T(8,128)(2,1)} %vd_hbm.1, bf16[2,256,1280]{2,1,0:T(8,128)(2,1)} %ck_hbm.1, bf16[2,256,1280]{2,1,0:T(8,128)(2,1)} %cv_hbm.1, s32[2]{0:T(128)} %len_hbm.1, f32[1280]{0:T(1024)} %gain_hbm.1), custom_call_target="tpu_custom_call" | custom-call | flops 1400000000 | bytes 8000000 | tf_op jit(solution)/shard_map/block_attention/pallas_call | solution.py:407
  60.7 1.4 %copy.9 = bf16[2,8,1280]{2,1,0:T(8,128)(2,1)} copy(bf16[2,8,1280]{2,1,0:T(8,128)(2,1)} %block_attention.1) | data formatting | bytes 81920

commit v6 on v5

--- a/solution.py
+++ b/solution.py
@@ -178,19 +178,23 @@
     def second_back(h, k, off):
         return remote(s2.at[h, off], r2.at[h, off - 1], r2s.at[h, off - 1], r2r.at[h, off - 1], along(stride_b(k), 4 - off))
 
-    def third_back(h, k, off):
-        return remote(s3.at[h, off], r3.at[h, off - 1], r3s.at[h, off - 1], r3r.at[h, off - 1], along(stride_a(k), 4 - off))
+    def third_back(n, off):
+        k = 2 * (n // 4)
+        return remote(s3.at[n, off], r3.at[n, off - 1], r3s.at[n, off - 1], r3r.at[n, off - 1], along(stride_a(k), 4 - off))
 
     scale = math.log2(math.e) / math.sqrt(DH)
 
-    def split(lse):
-        high = lse.astype(BF16).astype(F32)
-        middle = (lse - high).astype(BF16).astype(F32)
-        low = lse - high - middle
-        return jnp.concatenate([high, middle, low, jnp.zeros((10, DH), F32)], axis=0).astype(BF16)
-
-    def join(block):
-        rows = block.astype(F32)
+    def split(*lses):
+        rows = []
+        for lse in lses:
+            high = lse.astype(BF16).astype(F32)
+            middle = (lse - high).astype(BF16).astype(F32)
+            rows += [high, middle, lse - high - middle]
+        rows.append(jnp.zeros((16 - 6 * len(lses), DH), F32))
+        return jnp.concatenate(rows, axis=0).astype(BF16)
+
+    def join(block, i=0):
+        rows = block.astype(F32)[6 * i : 6 * i + 6]
         return rows[0:2] + rows[2:4] + rows[4:6]
 
     def attend(h, offs):
@@ -276,30 +280,33 @@
                 for i in (1, 2, 3):
                     acc += parts[i][32 * s : 32 * s + 32].astype(F32) * columns[:, 2 * i + s : 2 * i + s + 1]
                 merged.append(acc)
-            results.append((h, merged, split(lse)))
-        for h, merged, tail in results:
+            results.append((merged, lse))
+        for p, n in enumerate(pairs):
+            tail = split(results[2 * p][1], results[2 * p + 1][1])
             for i in range(4):
-                s3[h, i, 0:16] = jnp.concatenate([m[8 * i : 8 * i + 8] for m in merged], axis=0).astype(BF16)
-                s3[h, i, 16:32] = tail
-        for h, k in todo:
-            for off in FAR:
-                third_back(h, k, off).start()
+                for e in range(2):
+                    rows = [m[8 * i : 8 * i + 8] for m in results[2 * p + e][0]]
+                    s3[n, i, 16 * e : 16 * e + 16] = jnp.concatenate(rows, axis=0).astype(BF16)
+                s3[n, i, 32:48] = tail
+        for n in pairs:
+            for off in FAR:
+                third_back(n, off).start()
 
     def merge_third(*pairs):
-        todo = [entry for n in pairs for entry in pair(n)]
-        for h, k in todo:
-            for off in OFFS:
-                third_back(h, k, off).wait_recv()
+        for n in pairs:
+            for off in OFFS:
+                third_back(n, off).wait_recv()
         results = []
-        for h, k in todo:
-            parts = [s3.at[h, 0]] + [r3.at[h, off - 1] for off in (1, 2, 3)]
-            factors, _ = merge([shifted(join(part[16:32]), 8 * i) for i, part in enumerate(parts)])
-            columns = turned(factors)[0:8]
-            acc = jnp.zeros((16, DH), F32)
-            for i in range(4):
-                column = jnp.concatenate([columns[:, 2 * i + s : 2 * i + s + 1] for s in range(2)], axis=0)
-                acc += parts[i][0:16].astype(F32) * column
-            results.append((h, acc))
+        for n in pairs:
+            parts = [s3.at[n, 0]] + [r3.at[n, off - 1] for off in (1, 2, 3)]
+            for e, (h, _) in enumerate(pair(n)):
+                factors, _ = merge([shifted(join(part[32:48], e), 8 * i) for i, part in enumerate(parts)])
+                columns = turned(factors)[0:8]
+                acc = jnp.zeros((16, DH), F32)
+                for i in range(4):
+                    column = jnp.concatenate([columns[:, 2 * i + s : 2 * i + s + 1] for s in range(2)], axis=0)
+                    acc += parts[i][16 * e : 16 * e + 16].astype(F32) * column
+                results.append((h, acc))
         for h, acc in results:
             attended[h] = acc
 
@@ -360,8 +367,10 @@
                 ab_to_c(h, k, off).wait_send()
                 first_back(h, k, off).wait_send()
                 second_back(h, k, off).wait_send()
-                third_back(h, k, off).wait_send()
-
+
+    for n in range(STEPS):
+        for off in OFFS:
+            third_back(n, off).wait_send()
     for off in (1, 2, 3):
         norm(off).wait()
     squares = squares + nrecv[0] + nrecv[1] + nrecv[2]
@@ -389,8 +398,8 @@
         pltpu.VMEM((HEADS, 3, 272, DH), BF16),
         pltpu.VMEM((HEADS, 4, 80, DH), BF16),
         pltpu.VMEM((HEADS, 3, 80, DH), BF16),
-        pltpu.VMEM((HEADS, 4, 32, DH), BF16),
-        pltpu.VMEM((HEADS, 3, 32, DH), BF16),
+        pltpu.VMEM((STEPS, 4, 48, DH), BF16),
+        pltpu.VMEM((STEPS, 3, 48, DH), BF16),
         pltpu.VMEM((HEADS, 16, DH), F32),
         pltpu.VMEM((16, DH), F32),
         pltpu.VMEM((3, 16, DH), F32),

time: 62.3 us -> 61.7 us (level)
  no operation moved by 1% of the time
where the time goes in v6:
time: 61.7 us; the launch traced here: 61.5 us
  Pallas kernels  60.1 us (97%)
  local copies, waits for them, and re-layouts  1.4 us (2%)
    pallas_call x1, Pallas kernels, per_device(): pl.pallas_call(kernel, out_shape=jax.ShapeDtypeStruct(q_dec.shape, BF16),...  60.1 us
    unnamed x1, local copies, waits for them, and re-layouts  1.4 us

profile of v6, /device:TPU:1, one launch (start us, length us, event | category | flops | bytes accessed | tf_op | source)
XLA Modules:
  0.0 61.5 jit_solution(17058321228209787560)
XLA Ops:
  0.0 60.1 %block_attention.1 = bf16[2,8,1280]{2,1,0:T(8,128)(2,1)} custom-call(bf16[2,8,1280]{2,1,0:T(8,128)(2,1)} %q_hbm.1, bf16[2,8,1280]{2,1,0:T(8,128)(2,1)} %kd_hbm.1, bf16[2,8,1280]{2,1,0:T(8,128)(2,1)} %vd_hbm.1, bf16[2,256,1280]{2,1,0:T(8,128)(2,1)} %ck_hbm.1, bf16[2,256,1280]{2,1,0:T(8,128)(2,1)} %cv_hbm.1, s32[2]{0:T(128)} %len_hbm.1, f32[1280]{0:T(1024)} %gain_hbm.1), custom_call_target="tpu_custom_call" | custom-call | flops 1400000000 | bytes 8000000 | tf_op jit(solution)/shard_map/block_attention/pallas_call | solution.py:416
  60.1 1.4 %copy.9 = bf16[2,8,1280]{2,1,0:T(8,128)(2,1)} copy(bf16[2,8,1280]{2,1,0:T(8,128)(2,1)} %block_attention.1) | data formatting | bytes 81920

commit v7 on v6

--- a/solution.py
+++ b/solution.py
@@ -41,13 +41,14 @@
         here = (ctx // stride) % 4
         return (ctx + ((here + off) % 4 - here) * stride, tp)
 
+    loads[0].start()
     barrier = pltpu.get_barrier_semaphore()
     for off in (2, 1, 3):
         for name in "zyx":
             pl.semaphore_signal(barrier, inc=1, device_id=along(STRIDE[name], off), device_id_type=MESH)
         pl.semaphore_signal(barrier, inc=1, device_id=(ctx, (tp + off) % 4), device_id_type=MESH)
 
-    for load in loads:
+    for load in loads[1:]:
         load.start()
 
     loads[0].wait()

time: 61.7 us -> 61.6 us (level)
  no operation moved by 1% of the time
where the time goes in v7:
time: 61.6 us; the launch traced here: 61.4 us
  Pallas kernels  60 us (97%)
  local copies, waits for them, and re-layouts  1.4 us (2%)
    pallas_call x1, Pallas kernels, per_device(): pl.pallas_call(kernel, out_shape=jax.ShapeDtypeStruct(q_dec.shape, BF16),...  60 us
    unnamed x1, local copies, waits for them, and re-layouts  1.4 us

profile of v7, /device:TPU:1, one launch (start us, length us, event | category | flops | bytes accessed | tf_op | source)
XLA Modules:
  0.0 61.4 jit_solution(16882838779638801727)
XLA Ops:
  0.0 60.0 %block_attention.1 = bf16[2,8,1280]{2,1,0:T(8,128)(2,1)} custom-call(bf16[2,8,1280]{2,1,0:T(8,128)(2,1)} %q_hbm.1, bf16[2,8,1280]{2,1,0:T(8,128)(2,1)} %kd_hbm.1, bf16[2,8,1280]{2,1,0:T(8,128)(2,1)} %vd_hbm.1, bf16[2,256,1280]{2,1,0:T(8,128)(2,1)} %ck_hbm.1, bf16[2,256,1280]{2,1,0:T(8,128)(2,1)} %cv_hbm.1, s32[2]{0:T(128)} %len_hbm.1, f32[1280]{0:T(1024)} %gain_hbm.1), custom_call_target="tpu_custom_call" | custom-call | flops 1400000000 | bytes 8000000 | tf_op jit(solution)/shard_map/block_attention/pallas_call | solution.py:417
  60.0 1.4 %copy.9 = bf16[2,8,1280]{2,1,0:T(8,128)(2,1)} copy(bf16[2,8,1280]{2,1,0:T(8,128)(2,1)} %block_attention.1) | data formatting | bytes 81920
